TPU v7x, 128 devices: a whole 4x4x4 slice. The times are simulated.
128 devices in a mesh: row: 16 (over x, z), col: 8 (over y, core).
Axes of the slice: x: 4, y: 4, z: 4, core: 2. Of those that a mesh axis runs over, the one named last changes fastest.
Arguments:
- query_tiles: bfloat16 [512, 512, 512], P('row', 'col'), may hold values from -12 to 12
- key_tiles: bfloat16 [512, 512, 512], P('row', 'col'), may hold values from -12 to 12
- value_tiles: bfloat16 [512, 512, 512], P('row', 'col'), may hold values from -6 to 6
- out_grad: bfloat16 [512, 512, 512], P('row', 'col'), may hold values from -6 to 6
Outputs:
- attended: bfloat16 [512, 512, 512], P('row', 'col')
- query_grad: bfloat16 [512, 512, 512], P('row', 'col')
- key_grad: bfloat16 [512, 512, 512], P('row', 'col')
- value_grad: bfloat16 [512, 512, 512], P('row', 'col')
All inputs are finite; a program needn't handle non-finite values.
Results may differ from a plain program's by a relative error of at most 0.015.
Values may be sent and summed in bfloat16 or wider, within the bound.
A program may use at most 192 MiB of HBM per device.

v0:
```python
import jax
import jax.numpy as jnp
from jax import lax
from jax.sharding import PartitionSpec as P

H = 4


NEG_FILL = -1e30
ROW_SPECS = ("bqhe,bkhe->bhqk", "bhqk,bkhe->bqhe", "bhqk,bqhe->bkhe", (0, 2, 1), (0, 2, 1))
COLUMN_SPECS = ("qbhe,kbhe->bhqk", "bhqk,kbhe->qbhe", "bhqk,qbhe->kbhe", (2, 0, 1), (1, 2, 0))


def causal_mask(length, strict):
    query_pos = lax.broadcasted_iota(jnp.int32, (length, length), 0)
    key_pos = lax.broadcasted_iota(jnp.int32, (length, length), 1)
    if strict:
        return key_pos < query_pos
    return key_pos <= query_pos


def split_heads(array_in):
    return array_in.reshape(array_in.shape[:-1] + (H, array_in.shape[-1] // H))


def merge_heads(array_in):
    return array_in.reshape(array_in.shape[:-2] + (array_in.shape[-2] * array_in.shape[-1],))


def order_columns(array_in, row_count, col_count):
    rows_here, cols_here, last_width = array_in.shape
    narrow = cols_here // (row_count * col_count)
    grouped = array_in.reshape(rows_here, col_count, row_count, narrow, last_width)
    return jnp.transpose(grouped, (0, 2, 1, 3, 4)).reshape(rows_here, cols_here, last_width)


def unorder_stats(array_in, row_count, col_count):
    cols_here, rows_here, last_width = array_in.shape
    narrow = cols_here // (row_count * col_count)
    grouped = array_in.reshape(row_count, col_count, narrow, rows_here, last_width)
    ordered = jnp.transpose(grouped, (1, 0, 2, 3, 4)).reshape(cols_here, rows_here, last_width)
    return jnp.transpose(ordered, (1, 0, 2))


def attention_scores(query_heads, key_heads, spec_set):
    scale_factor = query_heads.shape[-1] ** (-0.5)
    return (
        jnp.einsum(spec_set[0], query_heads, key_heads, preferred_element_type=jnp.float32)
        * scale_factor
    )


def forward_part(query_heads, key_heads, value_heads, spec_set, strict):
    scores = attention_scores(query_heads, key_heads, spec_set)
    causal = causal_mask(scores.shape[-1], strict)
    top_score = jnp.max(jnp.where(causal, scores, NEG_FILL), axis=-1)
    weights = jnp.where(causal, jnp.exp(scores - top_score[..., None]), 0.0)
    weight_sum = jnp.maximum(jnp.sum(weights, axis=-1), 1.0)
    numerator = jnp.einsum(
        spec_set[1], weights.astype(jnp.bfloat16), value_heads, preferred_element_type=jnp.float32
    )
    partial_out = numerator / jnp.transpose(weight_sum, spec_set[3])[..., None]
    log_total = jnp.transpose(top_score + jnp.log(weight_sum), spec_set[3])
    return (partial_out.astype(jnp.bfloat16), log_total, scores)


def backward_part(
    query_heads, key_heads, value_heads, grad_heads, log_total, grad_dot, scores, spec_set, strict
):
    scores = attention_scores(query_heads, key_heads, spec_set)
    scale_factor = query_heads.shape[-1] ** (-0.5)
    causal = causal_mask(scores.shape[-1], strict)
    total_back = jnp.transpose(log_total, spec_set[4])
    weights = jnp.where(causal, jnp.exp(scores - total_back[..., None]), 0.0)
    weight_grad = jnp.einsum(
        spec_set[0], grad_heads, value_heads, preferred_element_type=jnp.float32
    )
    score_grad = weights * (weight_grad - jnp.transpose(grad_dot, spec_set[4])[..., None])
    weights_half = weights.astype(jnp.bfloat16)
    score_half = score_grad.astype(jnp.bfloat16)
    value_grad = jnp.einsum(
        spec_set[2], weights_half, grad_heads, preferred_element_type=jnp.float32
    )
    query_grad = (
        jnp.einsum(spec_set[1], score_half, key_heads, preferred_element_type=jnp.float32)
        * scale_factor
    )
    key_grad = (
        jnp.einsum(spec_set[2], score_half, query_heads, preferred_element_type=jnp.float32)
        * scale_factor
    )
    return (
        merge_heads(query_grad.astype(jnp.bfloat16)),
        merge_heads(key_grad.astype(jnp.bfloat16)),
        merge_heads(value_grad.astype(jnp.bfloat16)),
    )


def part_shares(first_total, second_total):
    top_total = jnp.maximum(first_total, second_total)
    log_total = top_total + jnp.log(
        jnp.exp(first_total - top_total) + jnp.exp(second_total - top_total)
    )
    return (jnp.exp(first_total - log_total), jnp.exp(second_total - log_total), log_total)


def shards(query_tiles, key_tiles, value_tiles, out_grad):
    row_count = lax.axis_size("row")
    col_count = lax.axis_size("col")
    row_side = (
        lax.all_to_all(query_tiles, "col", split_axis=0, concat_axis=1, tiled=True),
        lax.all_to_all(key_tiles, "col", split_axis=0, concat_axis=1, tiled=True),
        lax.all_to_all(value_tiles, "col", split_axis=0, concat_axis=1, tiled=True),
        lax.all_to_all(out_grad, "col", split_axis=0, concat_axis=1, tiled=True),
    )
    column_side = (
        lax.all_to_all(
            order_columns(row_side[0], row_count, col_count),
            ("row", "col"),
            split_axis=1,
            concat_axis=0,
            tiled=True,
        ),
        lax.all_to_all(
            order_columns(row_side[1], row_count, col_count),
            ("row", "col"),
            split_axis=1,
            concat_axis=0,
            tiled=True,
        ),
        lax.all_to_all(
            order_columns(row_side[2], row_count, col_count),
            ("row", "col"),
            split_axis=1,
            concat_axis=0,
            tiled=True,
        ),
        lax.all_to_all(
            order_columns(row_side[3], row_count, col_count),
            ("row", "col"),
            split_axis=1,
            concat_axis=0,
            tiled=True,
        ),
    )
    row_query, row_key, row_value, row_grad = [split_heads(array_in) for array_in in row_side]
    column_query, column_key, column_value, column_grad = [
        split_heads(array_in) for array_in in column_side
    ]
    row_out, row_total, row_scores = forward_part(row_query, row_key, row_value, ROW_SPECS, False)
    column_out, column_total, column_scores = forward_part(
        column_query, column_key, column_value, COLUMN_SPECS, True
    )
    row_dot = jnp.sum(row_grad.astype(jnp.float32) * row_out.astype(jnp.float32), axis=-1)
    column_dot = jnp.sum(column_grad.astype(jnp.float32) * column_out.astype(jnp.float32), axis=-1)
    crossed = (
        lax.all_to_all(
            order_columns(row_total, row_count, col_count),
            ("row", "col"),
            split_axis=1,
            concat_axis=0,
            tiled=True,
        ),
        lax.all_to_all(
            order_columns(row_dot, row_count, col_count),
            ("row", "col"),
            split_axis=1,
            concat_axis=0,
            tiled=True,
        ),
        lax.all_to_all(
            jnp.transpose(column_total, (1, 0, 2)),
            ("row", "col"),
            split_axis=1,
            concat_axis=0,
            tiled=True,
        ),
        lax.all_to_all(
            jnp.transpose(column_dot, (1, 0, 2)),
            ("row", "col"),
            split_axis=1,
            concat_axis=0,
            tiled=True,
        ),
    )
    far_row_total = crossed[0]
    far_row_dot = crossed[1]
    far_column_total = unorder_stats(crossed[2], row_count, col_count)
    far_column_dot = unorder_stats(crossed[3], row_count, col_count)
    row_share, column_far_share, row_log = part_shares(row_total, far_column_total)
    row_delta = row_share * row_dot + column_far_share * far_column_dot
    row_far_share, column_share, column_log = part_shares(far_row_total, column_total)
    column_delta = row_far_share * far_row_dot + column_share * column_dot
    row_keep, column_keep = (None, None)
    row_grads = backward_part(
        row_query, row_key, row_value, row_grad, row_log, row_delta, row_keep, ROW_SPECS, False
    )
    column_grads = backward_part(
        column_query,
        column_key,
        column_value,
        column_grad,
        column_log,
        column_delta,
        column_keep,
        COLUMN_SPECS,
        True,
    )
    row_weighted = merge_heads(
        (row_share[..., None] * row_out.astype(jnp.float32)).astype(jnp.bfloat16)
    )
    column_weighted = merge_heads(
        (column_share[..., None] * column_out.astype(jnp.float32)).astype(jnp.bfloat16)
    )
    row_back = (
        lax.all_to_all(row_weighted, "col", split_axis=1, concat_axis=0, tiled=True),
        lax.all_to_all(row_grads[0], "col", split_axis=1, concat_axis=0, tiled=True),
        lax.all_to_all(row_grads[1], "col", split_axis=1, concat_axis=0, tiled=True),
        lax.all_to_all(row_grads[2], "col", split_axis=1, concat_axis=0, tiled=True),
    )
    column_back = (
        lax.all_to_all(column_weighted, "row", split_axis=0, concat_axis=1, tiled=True),
        lax.all_to_all(column_grads[0], "row", split_axis=0, concat_axis=1, tiled=True),
        lax.all_to_all(column_grads[1], "row", split_axis=0, concat_axis=1, tiled=True),
        lax.all_to_all(column_grads[2], "row", split_axis=0, concat_axis=1, tiled=True),
    )
    results = [
        (row_back[member].astype(jnp.float32) + column_back[member].astype(jnp.float32)).astype(
            jnp.bfloat16
        )
        for member in range(4)
    ]
    return (results[0], results[1], results[2], results[3])


def solution(mesh):
    in_specs = (
        P("row", "col", None),
        P("row", "col", None),
        P("row", "col", None),
        P("row", "col", None),
    )
    out_specs = (
        P("row", "col", None),
        P("row", "col", None),
        P("row", "col", None),
        P("row", "col", None),
    )
    return jax.shard_map(shards, mesh=mesh, in_specs=in_specs, out_specs=out_specs, check_vma=False)
```

profile of v0, /device:TPU:8, one launch (start us, length us, event | category | flops | bytes accessed | tf_op | source)
XLA Modules:
  0.0 742.7 jit_solution(6403398943916567125)
XLA Ops:
  0.7 31.3 %all_to_all.258 = bf16[32,64,512]{2,1,0:T(8,128)(2,1)} all-to-all(bf16[32,64,512]{2,1,0:T(8,128)(2,1)} %param.4), channel_id=1, replica_groups=mesh['row'=16,'col'=8] {'col'}, dimensions={0} | all-to-all | bytes 4194304 | tf_op jit(solution)/shard_map/all_to_all | solution.py:111
  32.0 30.7 %all_to_all.259 = bf16[32,64,512]{2,1,0:T(8,128)(2,1)} all-to-all(bf16[32,64,512]{2,1,0:T(8,128)(2,1)S(1)} %copy-done.13), channel_id=1, replica_groups=mesh['row'=16,'col'=8] {'col'}, dimensions={0} | all-to-all | bytes 4194304 | tf_op jit(solution)/shard_map/all_to_all | solution.py:112
  62.7 30.7 %all_to_all.260 = bf16[32,64,512]{2,1,0:T(8,128)(2,1)} all-to-all(bf16[32,64,512]{2,1,0:T(8,128)(2,1)S(1)} %copy-done.14), channel_id=1, replica_groups=mesh['row'=16,'col'=8] {'col'}, dimensions={0} | all-to-all | bytes 4194304 | tf_op jit(solution)/shard_map/all_to_all | solution.py:113
  93.3 5.0 all-to-all-start.10
  104.2 19.9 %all-to-all-done.10 = bf16[32,64,512]{2,1,0:T(8,128)(2,1)S(1)} async-done(((bf16[32,64,512]{2,1,0:T(8,128)(2,1)}), bf16[32,64,512]{2,1,0:T(8,128)(2,1)S(1)}, u32[]{:S(2)}, u32[]{:S(2)}) %all-to-all-start.10) | async-done | bytes 2097184 | tf_op jit(solution)/shard_map/all_to_all | solution.py:114
  124.1 9.9 %all-to-all-start.3 = ((bf16[4,512,512]{2,0,1:T(4,128)(2,1)}), bf16[4,512,512]{2,0,1:T(4,128)(2,1)}, u32[]{:S(2)}, u32[]{:S(2)}) async-start(bf16[4,512,512]{2,0,1:T(4,128)(2,1)} %bitcast.319), calls=%async_computation.3 | async-start | bytes 4194304 | tf_op jit(solution)/shard_map/all_to_all | solution.py:124
  139.8 23.6 %all-to-all-done.3 = bf16[4,512,512]{2,0,1:T(4,128)(2,1)} async-done(((bf16[4,512,512]{2,0,1:T(4,128)(2,1)}), bf16[4,512,512]{2,0,1:T(4,128)(2,1)}, u32[]{:S(2)}, u32[]{:S(2)}) %all-to-all-start.3) | async-done | bytes 2097184 | tf_op jit(solution)/shard_map/all_to_all | solution.py:124
  163.4 6.2 all-to-all-start.2
  173.9 25.3 %all-to-all-done.2 = bf16[4,512,512]{2,0,1:T(4,128)(2,1)} async-done(((bf16[4,512,512]{2,0,1:T(4,128)(2,1)}), bf16[4,512,512]{2,0,1:T(4,128)(2,1)}, u32[]{:S(2)}, u32[]{:S(2)}) %all-to-all-start.2) | async-done | bytes 2097184 | tf_op jit(solution)/shard_map/all_to_all | solution.py:117
  199.2 6.6 all-to-all-start.11
  206.0 5.7 copy.345
  211.7 5.7 copy.344
  223.3 6.4 reshape.209
  229.7 6.4 reshape.208
  236.2 11.0 %select_reduce_fusion.1 = (f32[4,4,512]{2,1,0:T(4,128)S(1)}, f32[4,4,512,512]{2,3,1,0:T(8,128)}) fusion(pred[512,512]{0,1:T(8,128)(4,1)S(1)} %iota_compare_fusion.1, bf16[4,512,4,128]{1,3,2,0:T(8,128)(2,1)} %reshape.208, bf16[4,512,4,128]{1,3,2,0:T(8,128)(2,1)} %reshape.209), kind=kOutput, calls=%fused_computation.7 | convolution fusion | flops 1086316544 | bytes 21266432 | tf_op jit(solution)/shard_map/bqhe,bkhe->bhqk/dot_general | solution.py:48
  247.1 9.1 %fusion.1 = f32[4,4,512]{2,1,0:T(4,128)S(1)} fusion(f32[4,4,512,512]{2,3,1,0:T(8,128)} %get-tuple-element.17, f32[4,4,512]{2,1,0:T(4,128)S(1)} %get-tuple-element.16, pred[512,512]{0,1:T(8,128)(4,1)S(1)} %iota_compare_fusion.1), kind=kLoop, calls=%fused_computation.9 | loop fusion | flops 16769024 | bytes 17104896 | tf_op jit(solution)/shard_map/reduce_sum | solution.py:58
  264.5 4.3 copy.293
  277.1 4.2 copy.304
  281.4 10.7 %all-to-all-start.8 = ((bf16[4,512,512]{2,0,1:T(4,128)(2,1)}), bf16[4,512,512]{2,0,1:T(4,128)(2,1)}, u32[]{:S(2)}, u32[]{:S(2)}) async-start(bf16[4,512,512]{2,0,1:T(4,128)(2,1)} %bitcast.316), calls=%async_computation.8 | async-start | bytes 4194304 | tf_op jit(solution)/shard_map/all_to_all | solution.py:131
  292.1 11.0 %select_reduce_fusion = (f32[4,4,512]{2,1,0:T(4,128)S(1)}, f32[4,4,512,512]{2,3,1,0:T(8,128)}) fusion(pred[512,512]{0,1:T(8,128)(4,1)S(1)} %iota_compare_fusion, bf16[512,4,4,128]{0,3,2,1:T(8,128)(2,1)} %copy.304, bf16[512,4,4,128]{0,3,2,1:T(8,128)(2,1)} %copy.293), kind=kOutput, calls=%fused_computation.5 | convolution fusion | flops 1086316544 | bytes 21266432 | tf_op jit(solution)/shard_map/qbhe,kbhe->bhqk/dot_general | solution.py:48
  303.0 9.1 %fusion.3 = f32[4,4,512]{2,1,0:T(4,128)S(1)} fusion(f32[4,4,512,512]{2,3,1,0:T(8,128)} %get-tuple-element.19, f32[4,4,512]{2,1,0:T(4,128)S(1)} %get-tuple-element.18, pred[512,512]{0,1:T(8,128)(4,1)S(1)} %iota_compare_fusion), kind=kLoop, calls=%fused_computation.11 | loop fusion | flops 16769024 | bytes 17104896 | tf_op jit(solution)/shard_map/reduce_sum | solution.py:58
  314.1 7.2 all-to-all-done.8
  321.4 5.7 all-to-all-start.4
  333.6 6.5 reshape.210
  347.2 4.3 copy.274
  370.2 9.8 %all-to-all-start.7 = ((f32[4,512,4]{2,0,1:T(4,128)}), f32[4,512,4]{2,0,1:T(4,128)S(1)}, u32[]{:S(2)}, u32[]{:S(2)}) async-start(f32[4,512,4]{2,0,1:T(4,128)} %bitcast.35), calls=%async_computation.7 | async-start | bytes 2097152 | tf_op jit(solution)/shard_map/all_to_all | solution.py:157
  380.0 10.1 %fusion.31 = (f32[4,512,4]{1,2,0:T(4,128)S(1)}, bf16[4,512,4,128]{1,3,2,0:T(8,128)(2,1)}) fusion(bf16[4,512,4,128]{1,3,2,0:T(8,128)(2,1)} %reshape.210, f32[4,512,4]{1,2,0:T(4,128)S(1)} %get-tuple-element.4, f32[4,512,4]{1,2,0:T(4,128)S(1)} %copy-done.23, f32[4,4,512,512]{2,3,1,0:T(8,128)} %get-tuple-element.17, f32[4,4,512]{2,1,0:T(4,128)S(1)} %get-tuple-element.16, ...), kind=kOutput, calls=%fused_computation.39 | convolution fusion | flops 1098899456 | bytes 23461888 | tf_op jit(solution)/shard_map/bhqk,bkhe->bqhe/dot_general | solution.py:59
  398.6 6.6 all-to-all-start.14
  409.8 10.3 %fusion.33 = (f32[512,4,4]{0,2,1:T(4,128)S(1)}, bf16[512,4,4,128]{0,3,2,1:T(8,128)(2,1)}) fusion(bf16[512,4,4,128]{0,3,2,1:T(8,128)(2,1)} %copy.274, f32[512,4,4]{0,2,1:T(4,128)S(1)} %subtract_exponential_fusion, f32[512,4,4]{0,2,1:T(4,128)} %get-tuple-element.14, f32[4,4,512,512]{2,3,1,0:T(8,128)} %get-tuple-element.19, ...), kind=kOutput, calls=%fused_computation.41 | convolution fusion | flops 1098899456 | bytes 23461888 | tf_op jit(solution)/shard_map/bhqk,kbhe->qbhe/dot_general | solution.py:59
  423.9 7.5 %all-to-all-start.12 = ((f32[4,512,4]{2,0,1:T(4,128)}), f32[4,512,4]{2,0,1:T(4,128)S(1)}, u32[]{:S(2)}, u32[]{:S(2)}) async-start(f32[4,512,4]{2,0,1:T(4,128)} %copy.275), calls=%async_computation.12 | async-start | bytes 2097152 | tf_op jit(solution)/shard_map/all_to_all | solution.py:178
  431.3 4.5 copy.251
  435.9 14.1 %all-to-all-done.12 = f32[4,512,4]{2,0,1:T(4,128)S(1)} async-done(((f32[4,512,4]{2,0,1:T(4,128)}), f32[4,512,4]{2,0,1:T(4,128)S(1)}, u32[]{:S(2)}, u32[]{:S(2)}) %all-to-all-start.12) | async-done | bytes 32800 | tf_op jit(solution)/shard_map/all_to_all | solution.py:178
  450.9 5.2 all-to-all-start.6
  456.1 5.9 copy.336
  462.0 5.9 copy.278
  471.8 11.4 %fusion.44 = bf16[4,4,512,128]{2,3,1,0:T(8,128)(2,1)} fusion(bf16[4,512,4,128]{1,3,2,0:T(8,128)(2,1)} %reshape.210, f32[4,4,512,512]{2,3,1,0:T(8,128)} %get-tuple-element.17, f32[4,4,512]{2,1,0:T(4,128)} %get-tuple-element.12, pred[512,512]{0,1:T(8,128)(4,1)} %copy-done.11), kind=kOutput, calls=%fused_computation.68 | convolution fusion | flops 1091567616 | bytes 21266432 | tf_op jit(solution)/shard_map/bhqk,bqhe->bkhe/dot_general | solution.py:81
  483.2 4.5 copy.311
  487.7 4.8 all-to-all-start.18
  492.5 9.7 %multiply_convert_fusion.1 = bf16[4,4,512,512]{2,3,1,0:T(8,128)(2,1)S(1)} fusion(f32[4,4,512,512]{2,3,1,0:T(8,128)} %get-tuple-element.17, bf16[4,512,4,128]{1,3,2,0:T(8,128)(2,1)} %reshape.210, f32[4,4,512]{2,1,0:T(4,128)S(1)} %copy-done.22, f32[4,4,512]{2,1,0:T(4,128)S(1)} %copy-done.21, pred[512,512]{0,1:T(8,128)(4,1)} %copy-done.11, ...), kind=kOutput, calls=%fused_computation.2 | convolution fusion | flops 1098907648 | bytes 29687808 | tf_op jit(solution)/shard_map/bqhe,bkhe->bhqk/dot_general | solution.py:75
  502.2 7.3 multiply_convert_fusion.3
  509.5 4.7 copy.300
  518.4 5.7 all-to-all-start.16
  524.1 6.0 multiply_convert_fusion.5
  530.1 4.5 copy.282
  534.6 15.4 %all-to-all-done.16 = bf16[4,512,512]{2,0,1:T(4,128)(2,1)} async-done(((bf16[4,512,512]{2,0,1:T(4,128)(2,1)}), bf16[4,512,512]{2,0,1:T(4,128)(2,1)}, u32[]{:S(2)}, u32[]{:S(2)}) %all-to-all-start.16) | async-done | bytes 2097184 | tf_op jit(solution)/shard_map/all_to_all | solution.py:218
  550.0 5.2 all-to-all-start.13
  555.1 4.6 copy.341
  561.8 11.3 %fusion.47 = bf16[4,4,512,128]{2,3,1,0:T(8,128)(2,1)} fusion(bf16[512,4,4,128]{0,3,2,1:T(8,128)(2,1)} %copy.274, f32[4,4,512,512]{2,3,1,0:T(8,128)} %get-tuple-element.19, f32[4,4,512]{2,1,0:T(4,128)S(1)} %get-tuple-element.10, pred[512,512]{0,1:T(8,128)(4,1)S(1)} %iota_compare_fusion), kind=kOutput, calls=%fused_computation.69 | convolution fusion | flops 1091567616 | bytes 21266432 | tf_op jit(solution)/shard_map/bhqk,qbhe->kbhe/dot_general | solution.py:81
  573.0 4.5 copy.316
  580.9 4.4 all-to-all-start.19
  585.3 9.7 %multiply_convert_fusion = bf16[4,4,512,512]{2,3,1,0:T(8,128)(2,1)S(1)} fusion(f32[4,4,512,512]{2,3,1,0:T(8,128)} %get-tuple-element.19, bf16[512,4,4,128]{0,3,2,1:T(8,128)(2,1)} %copy.274, f32[4,4,512]{2,1,0:T(4,128)S(1)} %get-tuple-element.11, f32[4,4,512]{2,1,0:T(4,128)S(1)} %get-tuple-element.10, pred[512,512]{0,1:T(8,128)(4,1)S(1)} %iota_compare_fusion, ...), kind=kOutput, calls=%fused_computation | convolution fusion | flops 1098907648 | bytes 29687808 | tf_op jit(solution)/shard_map/qbhe,kbhe->bhqk/dot_general | solution.py:75
  595.1 7.3 multiply_convert_fusion.2
  602.4 4.6 copy.305
  607.1 8.8 %all-to-all-done.19 = bf16[512,4,512]{2,1,0:T(4,128)(2,1)} async-done(((bf16[512,4,512]{2,1,0:T(4,128)(2,1)}), bf16[512,4,512]{2,1,0:T(4,128)(2,1)}, u32[]{:S(2)}, u32[]{:S(2)}) %all-to-all-start.19) | async-done | bytes 2097184 | tf_op jit(solution)/shard_map/all_to_all | solution.py:225
  615.8 4.4 all-to-all-start.17
  620.3 6.0 multiply_convert_fusion.4
  626.3 4.5 copy.294
  630.8 17.4 %all-to-all-done.17 = bf16[512,4,512]{2,1,0:T(4,128)(2,1)} async-done(((bf16[512,4,512]{2,1,0:T(4,128)(2,1)}), bf16[512,4,512]{2,1,0:T(4,128)(2,1)}, u32[]{:S(2)}, u32[]{:S(2)}) %all-to-all-start.17) | async-done | bytes 2097184 | tf_op jit(solution)/shard_map/all_to_all | solution.py:224
  648.2 4.4 all-to-all-start.15
  652.6 4.5 copy.263
  661.0 19.2 %all-to-all-done.15 = bf16[512,4,512]{2,1,0:T(4,128)(2,1)} async-done(((bf16[512,4,512]{2,1,0:T(4,128)(2,1)}), bf16[512,4,512]{2,1,0:T(4,128)(2,1)}, u32[]{:S(2)}, u32[]{:S(2)}) %all-to-all-start.15) | async-done | bytes 2097184 | tf_op jit(solution)/shard_map/all_to_all | solution.py:223
  680.2 4.7 all-to-all-start.9
  718.7 13.1 %fusion.34 = (bf16[32,64,512]{2,1,0:T(8,128)(2,1)}, bf16[32,64,512]{2,1,0:T(8,128)(2,1)}) fusion(f32[8,4,64,512]{3,2,1,0:T(8,128)} %copy.313, f32[32,64,512]{2,0,1:T(8,128)} %bitcast.306, f32[32,64,512]{2,0,1:T(8,128)} %bitcast.305, f32[8,4,64,512]{3,2,1,0:T(8,128)} %copy.302), kind=kLoop, calls=%fused_computation.51 | loop fusion | flops 4194304 | bytes 20971520 | tf_op jit(solution)/shard_map/convert_element_type | solution.py:228
  731.8 10.5 %fusion.36 = (bf16[32,64,512]{2,1,0:T(8,128)(2,1)}, bf16[32,64,512]{2,1,0:T(8,128)(2,1)}) fusion(f32[8,4,64,512]{3,2,1,0:T(8,128)S(1)} %copy-done.3, f32[32,64,512]{2,0,1:T(8,128)} %bitcast.304, f32[32,64,512]{2,0,1:T(8,128)} %bitcast.307, f32[8,4,64,512]{3,2,1,0:T(8,128)S(1)} %copy-done.2), kind=kLoop, calls=%fused_computation.55 | loop fusion | flops 4194304 | bytes 20971520 | tf_op jit(solution)/shard_map/convert_element_type | solution.py:228
  (120 shorter events, 141.4 us)
Async XLA Ops:
  0.6 31.4 %copy-start.13 = (bf16[32,64,512]{2,1,0:T(8,128)(2,1)S(1)}, bf16[32,64,512]{2,1,0:T(8,128)(2,1)}, u32[]{:S(2)}) copy-start(bf16[32,64,512]{2,1,0:T(8,128)(2,1)} %param.5) | copy-start | bytes 6291460
  0.6 62.0 %copy-start.14 = (bf16[32,64,512]{2,1,0:T(8,128)(2,1)S(1)}, bf16[32,64,512]{2,1,0:T(8,128)(2,1)}, u32[]{:S(2)}) copy-start(bf16[32,64,512]{2,1,0:T(8,128)(2,1)} %param.6) | copy-start | bytes 6291460
  93.3 30.7 %all-to-all-start.10 = ((bf16[32,64,512]{2,1,0:T(8,128)(2,1)}), bf16[32,64,512]{2,1,0:T(8,128)(2,1)S(1)}, u32[]{:S(2)}, u32[]{:S(2)}) async-start(bf16[32,64,512]{2,1,0:T(8,128)(2,1)} %param.7), calls=%async_computation.10 | async-start | bytes 4194304 | tf_op jit(solution)/shard_map/all_to_all | solution.py:114
  124.1 39.3 %all-to-all-start.3 = ((bf16[4,512,512]{2,0,1:T(4,128)(2,1)}), bf16[4,512,512]{2,0,1:T(4,128)(2,1)}, u32[]{:S(2)}, u32[]{:S(2)}) async-start(bf16[4,512,512]{2,0,1:T(4,128)(2,1)} %bitcast.319), calls=%async_computation.3 | async-start | bytes 4194304 | tf_op jit(solution)/shard_map/all_to_all | solution.py:124
  163.4 35.8 %all-to-all-start.2 = ((bf16[4,512,512]{2,0,1:T(4,128)(2,1)}), bf16[4,512,512]{2,0,1:T(4,128)(2,1)}, u32[]{:S(2)}, u32[]{:S(2)}) async-start(bf16[4,512,512]{2,0,1:T(4,128)(2,1)} %bitcast.318), calls=%async_computation.2 | async-start | bytes 4194304 | tf_op jit(solution)/shard_map/all_to_all | solution.py:117
  199.2 82.1 %all-to-all-start.11 = ((bf16[4,512,512]{2,0,1:T(4,128)(2,1)}), bf16[4,512,512]{2,0,1:T(4,128)(2,1)}, u32[]{:S(2)}, u32[]{:S(2)}) async-start(bf16[4,512,512]{2,0,1:T(4,128)(2,1)} %bitcast.317), calls=%async_computation.11 | async-start | bytes 4194304 | tf_op jit(solution)/shard_map/all_to_all | solution.py:138
  205.9 41.2 %copy-start.11 = (pred[512,512]{0,1:T(8,128)(4,1)}, pred[512,512]{0,1:T(8,128)(4,1)S(1)}, u32[]{:S(2)}) copy-start(pred[512,512]{0,1:T(8,128)(4,1)S(1)} %iota_compare_fusion.1) | copy-start | bytes 786436
  281.4 40.0 %all-to-all-start.8 = ((bf16[4,512,512]{2,0,1:T(4,128)(2,1)}), bf16[4,512,512]{2,0,1:T(4,128)(2,1)}, u32[]{:S(2)}, u32[]{:S(2)}) async-start(bf16[4,512,512]{2,0,1:T(4,128)(2,1)} %bitcast.316), calls=%async_computation.8 | async-start | bytes 4194304 | tf_op jit(solution)/shard_map/all_to_all | solution.py:131
  321.4 35.1 %all-to-all-start.4 = ((f32[4,512,4]{2,0,1:T(4,128)}), f32[4,512,4]{2,0,1:T(4,128)S(1)}, u32[]{:S(2)}, u32[]{:S(2)}) async-start(f32[4,512,4]{2,0,1:T(4,128)} %copy.244), calls=%async_computation.4 | async-start | bytes 2097152 | tf_op jit(solution)/shard_map/all_to_all | solution.py:171
  360.3 19.7 %copy-start.12 = (pred[512,512]{0,1:T(8,128)(4,1)S(1)}, pred[512,512]{0,1:T(8,128)(4,1)}, u32[]{:S(2)}) copy-start(pred[512,512]{0,1:T(8,128)(4,1)} %copy-done.11) | copy-start | bytes 786436
  360.3 19.7 %copy-start.23 = (f32[4,512,4]{1,2,0:T(4,128)S(1)}, f32[4,512,4]{1,2,0:T(4,128)}, u32[]{:S(2)}) copy-start(f32[4,512,4]{1,2,0:T(4,128)} %maximum_bitcast_fusion.1) | copy-start | bytes 98308
  364.8 25.4 %copy-start.15 = (f32[512,4,4]{0,2,1:T(4,128)}, f32[512,4,4]{0,2,1:T(4,128)S(1)}, u32[]{:S(2)}) copy-start(f32[512,4,4]{0,2,1:T(4,128)S(1)} %reshape.169) | copy-start | bytes 98308
  370.2 28.4 %all-to-all-start.7 = ((f32[4,512,4]{2,0,1:T(4,128)}), f32[4,512,4]{2,0,1:T(4,128)S(1)}, u32[]{:S(2)}, u32[]{:S(2)}) async-start(f32[4,512,4]{2,0,1:T(4,128)} %bitcast.35), calls=%async_computation.7 | async-start | bytes 2097152 | tf_op jit(solution)/shard_map/all_to_all | solution.py:157
  390.2 8.4 %copy-start.20 = (f32[4,512,4]{1,2,0:T(4,128)}, f32[4,512,4]{1,2,0:T(4,128)S(1)}, u32[]{:S(2)}) copy-start(f32[4,512,4]{1,2,0:T(4,128)S(1)} %get-tuple-element.6) | copy-start | bytes 98308
  398.6 25.2 %all-to-all-start.14 = ((f32[4,512,4]{2,0,1:T(4,128)}), f32[4,512,4]{2,0,1:T(4,128)S(1)}, u32[]{:S(2)}, u32[]{:S(2)}) async-start(f32[4,512,4]{2,0,1:T(4,128)} %bitcast.74), calls=%async_computation.14 | async-start | bytes 2097152 | tf_op jit(solution)/shard_map/all_to_all | solution.py:164
  409.7 10.4 %copy-start.16 = (f32[512,4,4]{0,2,1:T(4,128)}, f32[512,4,4]{0,2,1:T(4,128)S(1)}, u32[]{:S(2)}) copy-start(f32[512,4,4]{0,2,1:T(4,128)S(1)} %all_to_all.214) | copy-start | bytes 98308
  420.2 3.7 copy-start.18
  423.9 26.1 %all-to-all-start.12 = ((f32[4,512,4]{2,0,1:T(4,128)}), f32[4,512,4]{2,0,1:T(4,128)S(1)}, u32[]{:S(2)}, u32[]{:S(2)}) async-start(f32[4,512,4]{2,0,1:T(4,128)} %copy.275), calls=%async_computation.12 | async-start | bytes 2097152 | tf_op jit(solution)/shard_map/all_to_all | solution.py:178
  449.9 1.0 copy-start.10
  450.9 36.8 %all-to-all-start.6 = ((bf16[4,512,512]{2,0,1:T(4,128)(2,1)}), bf16[4,512,512]{2,0,1:T(4,128)(2,1)S(1)}, u32[]{:S(2)}, u32[]{:S(2)}) async-start(bf16[4,512,512]{2,0,1:T(4,128)(2,1)} %copy.251), calls=%async_computation.6 | async-start | bytes 4194304 | tf_op jit(solution)/shard_map/all_to_all | solution.py:216
  483.2 9.3 %copy-start.21 = (f32[4,4,512]{2,1,0:T(4,128)S(1)}, f32[4,4,512]{2,1,0:T(4,128)}, u32[]{:S(2)}) copy-start(f32[4,4,512]{2,1,0:T(4,128)} %get-tuple-element.12) | copy-start | bytes 98308
  483.2 9.3 %copy-start.22 = (f32[4,4,512]{2,1,0:T(4,128)S(1)}, f32[4,4,512]{2,1,0:T(4,128)}, u32[]{:S(2)}) copy-start(f32[4,4,512]{2,1,0:T(4,128)} %get-tuple-element.13) | copy-start | bytes 98308
  487.7 14.5 %copy-start.6 = (bf16[4,512,512]{2,0,1:T(4,128)(2,1)}, bf16[4,512,512]{2,0,1:T(4,128)(2,1)S(1)}, u32[]{:S(2)}) copy-start(bf16[4,512,512]{2,0,1:T(4,128)(2,1)S(1)} %all-to-all-done.6) | copy-start | bytes 6291460
  487.7 30.7 %all-to-all-start.18 = ((bf16[4,512,512]{2,0,1:T(4,128)(2,1)}), bf16[4,512,512]{2,0,1:T(4,128)(2,1)}, u32[]{:S(2)}, u32[]{:S(2)}) async-start(bf16[4,512,512]{2,0,1:T(4,128)(2,1)} %copy.311), calls=%async_computation.18 | async-start | bytes 4194304 | tf_op jit(solution)/shard_map/all_to_all | solution.py:219
  502.2 7.3 copy-start.4
  509.5 14.6 %copy-start = (bf16[4,512,4,128]{1,3,2,0:T(8,128)(2,1)S(1)}, bf16[4,512,4,128]{1,3,2,0:T(8,128)(2,1)}, u32[]{:S(2)}) copy-start(bf16[4,512,4,128]{1,3,2,0:T(8,128)(2,1)} %reshape.209) | copy-start | bytes 6291460
  518.4 31.6 %all-to-all-start.16 = ((bf16[4,512,512]{2,0,1:T(4,128)(2,1)}), bf16[4,512,512]{2,0,1:T(4,128)(2,1)}, u32[]{:S(2)}, u32[]{:S(2)}) async-start(bf16[4,512,512]{2,0,1:T(4,128)(2,1)} %copy.300), calls=%async_computation.16 | async-start | bytes 4194304 | tf_op jit(solution)/shard_map/all_to_all | solution.py:218
  534.6 27.1 %copy-start.17 = (f32[512,4,4]{0,2,1:T(4,128)S(1)}, f32[512,4,4]{0,2,1:T(4,128)}, u32[]{:S(2)}) copy-start(f32[512,4,4]{0,2,1:T(4,128)} %copy-done.16) | copy-start | bytes 98308
  534.6 27.1 %copy-start.19 = (f32[512,4,4]{0,2,1:T(4,128)S(1)}, f32[512,4,4]{0,2,1:T(4,128)}, u32[]{:S(2)}) copy-start(f32[512,4,4]{0,2,1:T(4,128)} %copy-done.18) | copy-start | bytes 98308
  550.0 30.9 %all-to-all-start.13 = ((bf16[4,512,512]{2,0,1:T(4,128)(2,1)}), bf16[4,512,512]{2,0,1:T(4,128)(2,1)S(1)}, u32[]{:S(2)}, u32[]{:S(2)}) async-start(bf16[4,512,512]{2,0,1:T(4,128)(2,1)} %copy.282), calls=%async_computation.13 | async-start | bytes 4194304 | tf_op jit(solution)/shard_map/all_to_all | solution.py:217
  580.9 14.2 %copy-start.8 = (bf16[4,512,512]{2,0,1:T(4,128)(2,1)}, bf16[4,512,512]{2,0,1:T(4,128)(2,1)S(1)}, u32[]{:S(2)}) copy-start(bf16[4,512,512]{2,0,1:T(4,128)(2,1)S(1)} %all-to-all-done.13) | copy-start | bytes 6291460
  580.9 35.0 %all-to-all-start.19 = ((bf16[512,4,512]{2,1,0:T(4,128)(2,1)}), bf16[512,4,512]{2,1,0:T(4,128)(2,1)}, u32[]{:S(2)}, u32[]{:S(2)}) async-start(bf16[512,4,512]{2,1,0:T(4,128)(2,1)} %copy.316), calls=%async_computation.19 | async-start | bytes 4194304 | tf_op jit(solution)/shard_map/all_to_all | solution.py:225
  595.1 7.3 copy-start.5
  602.4 17.9 %copy-start.1 = (bf16[512,4,4,128]{0,3,2,1:T(8,128)(2,1)S(1)}, bf16[512,4,4,128]{0,3,2,1:T(8,128)(2,1)}, u32[]{:S(2)}) copy-start(bf16[512,4,4,128]{0,3,2,1:T(8,128)(2,1)} %copy.293) | copy-start | bytes 6291460
  615.8 32.3 %all-to-all-start.17 = ((bf16[512,4,512]{2,1,0:T(4,128)(2,1)}), bf16[512,4,512]{2,1,0:T(4,128)(2,1)}, u32[]{:S(2)}, u32[]{:S(2)}) async-start(bf16[512,4,512]{2,1,0:T(4,128)(2,1)} %copy.305), calls=%async_computation.17 | async-start | bytes 4194304 | tf_op jit(solution)/shard_map/all_to_all | solution.py:224
  630.8 26.3 %copy-start.7 = (bf16[4,512,512]{2,0,1:T(4,128)(2,1)S(1)}, bf16[4,512,512]{2,0,1:T(4,128)(2,1)}, u32[]{:S(2)}) copy-start(bf16[4,512,512]{2,0,1:T(4,128)(2,1)} %copy-done.6) | copy-start | bytes 6291460
  648.2 32.1 %all-to-all-start.15 = ((bf16[512,4,512]{2,1,0:T(4,128)(2,1)}), bf16[512,4,512]{2,1,0:T(4,128)(2,1)}, u32[]{:S(2)}, u32[]{:S(2)}) async-start(bf16[512,4,512]{2,1,0:T(4,128)(2,1)} %copy.294), calls=%async_computation.15 | async-start | bytes 4194304 | tf_op jit(solution)/shard_map/all_to_all | solution.py:223
  658.1 2.5 copy-start.9
  680.2 33.3 %all-to-all-start.9 = ((bf16[512,4,512]{2,1,0:T(4,128)(2,1)}), bf16[512,4,512]{2,1,0:T(4,128)(2,1)}, u32[]{:S(2)}, u32[]{:S(2)}) async-start(bf16[512,4,512]{2,1,0:T(4,128)(2,1)} %copy.263), calls=%async_computation.9 | async-start | bytes 4194304 | tf_op jit(solution)/shard_map/all_to_all | solution.py:222
  718.7 13.1 %copy-start.2 = (f32[8,4,64,512]{3,2,1,0:T(8,128)S(1)}, f32[8,4,64,512]{3,2,1,0:T(8,128)}, u32[]{:S(2)}) copy-start(f32[8,4,64,512]{3,2,1,0:T(8,128)} %copy.253) | copy-start | bytes 12582916
  718.7 13.1 %copy-start.3 = (f32[8,4,64,512]{3,2,1,0:T(8,128)S(1)}, f32[8,4,64,512]{3,2,1,0:T(8,128)}, u32[]{:S(2)}) copy-start(f32[8,4,64,512]{3,2,1,0:T(8,128)} %copy.284) | copy-start | bytes 12582916
where the time goes:
time: 756 us; the launch traced here: 743 us
  local copies, waits for them, and re-layouts  217 us (29%)
  waiting for transfers between devices  164 us (22%)
  matrix products  111 us (15%)
  starting transfers between devices  107 us (14%)
  blocking collectives  92.7 us (12%)
  other arithmetic  49.5 us (7%)
    reshape x14, local copies, waits for them, and re-layouts, split_heads(): return array_in.reshape(array_in.shape[:-1] + (H, array_in.shape[-1] // H))  62.5 us
    reshape x8, local copies, waits for them, and re-layouts, merge_heads(): array_in.reshape(array_in.shape[:-2] + (array_in.shape[-2] * array_in.sha...  36.3 us
    all_to_all x1, blocking collectives, shards(): lax.all_to_all(query_tiles, 'col', split_axis=0, concat_axis=1, tiled=True)  31.3 us
    all_to_all x1, blocking collectives, shards(): lax.all_to_all(value_tiles, 'col', split_axis=0, concat_axis=1, tiled=True)  30.7 us
    all_to_all x1, blocking collectives, shards(): lax.all_to_all(key_tiles, 'col', split_axis=0, concat_axis=1, tiled=True)  30.7 us
    all_to_all x1, waiting for transfers between devices, shards(): lax.all_to_all(order_columns(row_side[0], row_count, col_count), ('row',...  25.3 us
    all_to_all x1, waiting for transfers between devices, shards(): lax.all_to_all(order_columns(row_side[1], row_count, col_count), ('row',...  23.6 us
    convert_element_type x2, other arithmetic, shards(): (row_back[member].astype(jnp.float32) + column_back[member].astype(jnp.fl...  23.6 us
  transfers between devices with their start and end apart: 17, of which 13 were waited for; matrix products, arithmetic and copies ran while one was open for 45% of the time, Pallas kernels for 0%

commit v1 on v0

v1 whole, which is shorter than its diff:
```python
import functools

import jax
import jax.numpy as jnp
from jax import lax
from jax.experimental import pallas as pl
from jax.experimental.pallas import tpu as pltpu
from jax.sharding import PartitionSpec as P

H = 4
E = 128
G = 512
ROWS = 32
COLS = 64
NR = 16
NC = 8
K = 4
HALF = 256
LOG2E = 1.4426950408889634
SCALE = E ** (-0.5)
NEG = -1e30
MESH = pl.DeviceIdType.MESH
F32 = jnp.float32
BF16 = jnp.bfloat16


def dot_nn(a, b):
    return lax.dot_general(a, b, (((1,), (0,)), ((), ())), preferred_element_type=F32)


def dot_nt(a, b):
    return lax.dot_general(a, b, (((1,), (1,)), ((), ())), preferred_element_type=F32)


def dot_tn(a, b):
    return lax.dot_general(a, b, (((0,), (0,)), ((), ())), preferred_element_type=F32)


def swap_matrix():
    to = lax.broadcasted_iota(jnp.int32, (HALF, HALF), 0)
    of = lax.broadcasted_iota(jnp.int32, (HALF, HALF), 1)
    match = of == (to % 16) * 16 + to // 16
    return jnp.where(match, 1.0, 0.0).astype(BF16)


def kernel(
    q_in, k_in, v_in, g_in, row_back, col_back,
    xs, xt, ab, perm, st, so, rs, cs, mr, mc, rr, cr, mm, pr, pc, ct, lt,
    load_sem, in_send, in_recv, out_send, out_recv, stat_send, stat_recv, merged_send, merged_recv,
):
    me_r = lax.axis_index("row")
    me_c = lax.axis_index("col")
    core = lax.rem(me_c, 2)
    me_z = lax.rem(me_r, 4)
    inputs = (q_in, k_in, v_in, g_in)

    def row_peer(d):
        return lax.rem(me_c + d, NC)

    def col_peer(d):
        return lax.rem(me_r + d, NR)

    def load(h):
        return [
            pltpu.make_async_copy(
                inputs[a].at[:, :, pl.ds(pl.multiple_of(h * E, E), E)], xs.at[h, a], load_sem.at[h, a]
            )
            for a in range(4)
        ]

    for h in range(H):
        for copy in load(h):
            copy.start()

    barrier = pltpu.get_barrier_semaphore()

    @pl.loop(1, NC)
    def _(d):
        pl.semaphore_signal(barrier, inc=1, device_id=(me_r, row_peer(d)), device_id_type=MESH)

    @pl.loop(1, NR)
    def _(d):
        pl.semaphore_signal(barrier, inc=1, device_id=(col_peer(d), me_c), device_id_type=MESH)

    perm[...] = swap_matrix()
    st[...] = jnp.zeros_like(st)
    lt[...] = jnp.zeros_like(lt)
    pl.semaphore_wait(barrier, NC + NR - 2)

    def send_in(h):
        for copy in load(h):
            copy.wait()

        def row_src(dst):
            return xs.at[h, :, pl.ds(dst * K, K)]

        row_dst = ab.at[h, :, pl.ds(0, K), pl.ds(pl.multiple_of(me_c * COLS, COLS), COLS)]

        @pl.loop(1, NC)
        def _(d):
            dst = row_peer(d)
            pltpu.make_async_remote_copy(
                src_ref=row_src(dst), dst_ref=row_dst, send_sem=in_send.at[0], recv_sem=in_recv.at[h, 0],
                device_id=(me_r, dst), device_id_type=MESH,
            ).start()

        pltpu.make_async_copy(row_src(me_c), row_dst, in_recv.at[h, 0]).start()

        @pl.loop(0, 4)
        def _(a):
            for cb in range(COLS // 16):
                for rb in range(ROWS // 16):
                    block = xs[h, a, rb * 16:rb * 16 + 16, cb * 16:cb * 16 + 16, :]
                    moved = dot_nn(perm[...], block.reshape(HALF, E)).astype(BF16)
                    xt[h, a, cb * 16:cb * 16 + 16, rb * 16:rb * 16 + 16, :] = moved.reshape(16, 16, E)

        def col_src(dst):
            return xt.at[h, :, pl.ds(dst * K, K)]

        col_dst = ab.at[h, :, pl.ds(K, K), pl.ds(pl.multiple_of(me_r * ROWS, ROWS), ROWS)]

        @pl.loop(1, NR)
        def _(d):
            dst = col_peer(d)
            pltpu.make_async_remote_copy(
                src_ref=col_src(dst), dst_ref=col_dst, send_sem=in_send.at[1], recv_sem=in_recv.at[h, 1],
                device_id=(dst, me_c), device_id_type=MESH,
            ).start()

        pltpu.make_async_copy(col_src(me_r), col_dst, in_recv.at[h, 1]).start()

    def forward(h):
        lane = lax.broadcasted_iota(jnp.int32, (HALF, E), 1)
        q_pos = lax.broadcasted_iota(jnp.int32, (HALF, HALF), 0)
        k_pos = lax.broadcasted_iota(jnp.int32, (HALF, HALF), 1)

        for part in range(2):
            here = ab.at[h, :, pl.ds(part * K, K)]
            pltpu.make_async_copy(here, here, in_recv.at[h, part]).wait()

            @pl.loop(0, K)
            def _(k):
                i = part * K + k
                allowed = k_pos <= q_pos - part
                for qb in range(2):
                    rows = pl.ds(qb * HALF, HALF)
                    query = ab[h, 0, i, rows, :]
                    scores = [
                        dot_nt(query, ab[h, 1, i, pl.ds(kb * HALF, HALF), :]) * (SCALE * LOG2E)
                        for kb in range(qb + 1)
                    ]
                    scores[qb] = jnp.where(allowed, scores[qb], NEG)
                    top = scores[0].max(axis=-1, keepdims=True)
                    for s in scores[1:]:
                        top = jnp.maximum(top, s.max(axis=-1, keepdims=True))
                    top = jnp.maximum(top, 0.1 * NEG)
                    weights = [jnp.exp2(s - top) for s in scores]
                    total = weights[0].sum(axis=-1, keepdims=True)
                    for w in weights[1:]:
                        total = total + w.sum(axis=-1, keepdims=True)
                    total = jnp.maximum(total, 1.0)
                    numer = dot_nn(weights[0].astype(BF16), ab[h, 2, i, pl.ds(0, HALF), :])
                    if qb:
                        numer = numer + dot_nn(weights[1].astype(BF16), ab[h, 2, i, pl.ds(HALF, HALF), :])
                    out = (numer / total).astype(BF16).astype(F32)
                    product = (ab[h, 3, i, rows, :].astype(F32) * out).sum(axis=-1, keepdims=True)
                    log_part = top + jnp.log2(total)
                    base = part * 8 + k
                    st[rows, :] = jnp.where(
                        lane == base, log_part, jnp.where(lane == base + 4, product, st[rows, :])
                    )

        for b in range(4):
            block = st[b * E:(b + 1) * E, :].T
            so[h, :, b * E:(b + 1) * E] = block[:16, :]

        def row_stat(dst):
            return so.at[h, pl.ds(0, 8), pl.ds(pl.multiple_of((dst // 2) * E, E), E)]

        def col_stat(dst):
            return so.at[h, pl.ds(8, 8), pl.ds(pl.multiple_of((dst // 4) * E, E), E)]

        @pl.loop(1, NC)
        def _(d):
            dst = row_peer(d)
            pltpu.make_async_remote_copy(
                src_ref=row_stat(dst), dst_ref=rs.at[h, me_c], send_sem=stat_send.at[0],
                recv_sem=stat_recv.at[h, 0], device_id=(me_r, dst), device_id_type=MESH,
            ).start()

        pltpu.make_async_copy(row_stat(me_c), rs.at[h, me_c], stat_recv.at[h, 0]).start()

        @pl.loop(1, NR)
        def _(d):
            dst = col_peer(d)
            pltpu.make_async_remote_copy(
                src_ref=col_stat(dst), dst_ref=cs.at[h, me_r], send_sem=stat_send.at[1],
                recv_sem=stat_recv.at[h, 1], device_id=(dst, me_c), device_id_type=MESH,
            ).start()

        pltpu.make_async_copy(col_stat(me_r), cs.at[h, me_r], stat_recv.at[h, 1]).start()

    def merge(h):
        pltpu.make_async_copy(rs.at[h], rs.at[h], stat_recv.at[h, 0]).wait()
        pltpu.make_async_copy(cs.at[h], cs.at[h], stat_recv.at[h, 1]).wait()
        row_values = []
        col_values = []
        for s in range(2):
            for d in range(NC):
                pr[s, 4 * d:4 * d + 4, :] = rs[h, d, 4 * s:4 * s + 4, :]
            for j in range(NR):
                pc[s, 4 * j:4 * j + 4, :] = cs[h, j, 4 * s:4 * s + 4, :]
                pc[s, COLS + 4 * j:COLS + 4 * j + 4, :] = cs[h, j, 4 * s:4 * s + 4, :]
            ct[s] = pc[s].T
            row_values.append(pr[s])
            col_values.append(ct[s, pl.ds(pl.multiple_of(me_z * ROWS, ROWS), ROWS), :])
        top = jnp.maximum(row_values[0], col_values[0])
        log_total = top + jnp.log2(jnp.exp2(row_values[0] - top) + jnp.exp2(col_values[0] - top))
        delta = (
            jnp.exp2(row_values[0] - log_total) * row_values[1]
            + jnp.exp2(col_values[0] - log_total) * col_values[1]
        )
        for s, value in enumerate((log_total, delta)):
            pr[s] = value
            lt[s, pl.ds(pl.multiple_of(me_z * ROWS, ROWS), ROWS), :] = value
            turned = lt[s].T
            pc[s, :COLS, :] = jnp.where(core == 0, turned[:COLS], turned[COLS:])
            for d in range(NC):
                mr[h, d, 4 * s:4 * s + 4, :] = pr[s, 4 * d:4 * d + 4, :]
            for j in range(NR):
                mc[h, j, 4 * s:4 * s + 4, :] = pc[s, 4 * j:4 * j + 4, :]

        @pl.loop(1, NC)
        def _(d):
            dst = row_peer(d)
            pltpu.make_async_remote_copy(
                src_ref=mr.at[h, dst], dst_ref=rr.at[h, me_c], send_sem=merged_send.at[0],
                recv_sem=merged_recv.at[h, 0], device_id=(me_r, dst), device_id_type=MESH,
            ).start()

        pltpu.make_async_copy(mr.at[h, me_c], rr.at[h, me_c], merged_recv.at[h, 0]).start()

        @pl.loop(1, NR)
        def _(d):
            dst = col_peer(d)
            pltpu.make_async_remote_copy(
                src_ref=mc.at[h, dst], dst_ref=cr.at[h, me_r], send_sem=merged_send.at[1],
                recv_sem=merged_recv.at[h, 1], device_id=(dst, me_c), device_id_type=MESH,
            ).start()

        pltpu.make_async_copy(mc.at[h, me_r], cr.at[h, me_r], merged_recv.at[h, 1]).start()

    def backward(h):
        pltpu.make_async_copy(rr.at[h], rr.at[h], merged_recv.at[h, 0]).wait()
        pltpu.make_async_copy(cr.at[h], cr.at[h], merged_recv.at[h, 1]).wait()
        lane = lax.broadcasted_iota(jnp.int32, (8, E), 1)
        for y in range(4):
            mm[0:8, y * E:(y + 1) * E] = jnp.where(lane < COLS, rr[h, 2 * y], rr[h, 2 * y + 1])
            tile = cr[h, 4 * y]
            for z in range(1, 4):
                tile = jnp.where(lane >= z * ROWS, cr[h, 4 * y + z], tile)
            mm[8:16, y * E:(y + 1) * E] = tile

        k_pos = lax.broadcasted_iota(jnp.int32, (HALF, HALF), 0)
        q_pos = lax.broadcasted_iota(jnp.int32, (HALF, HALF), 1)

        for part in range(2):

            @pl.loop(0, K)
            def _(k):
                i = part * K + k
                allowed = k_pos <= q_pos - part
                key_grads = [None, None]
                value_grads = [None, None]
                for qb in range(2):
                    rows = pl.ds(qb * HALF, HALF)
                    query = ab[h, 0, i, rows, :]
                    grad = ab[h, 3, i, rows, :]
                    log_total = mm[pl.ds(part * 8 + k, 1), rows]
                    delta = mm[pl.ds(part * 8 + 4 + k, 1), rows]
                    query_grad = None
                    out = None
                    for kb in range(qb + 1):
                        keys = ab[h, 1, i, pl.ds(kb * HALF, HALF), :]
                        values = ab[h, 2, i, pl.ds(kb * HALF, HALF), :]
                        scores = dot_nt(keys, query) * (SCALE * LOG2E)
                        if kb == qb:
                            scores = jnp.where(allowed, scores, NEG)
                        probs = jnp.exp2(scores - log_total)
                        score_grad = probs * (dot_nt(values, grad) - delta)
                        probs_half = probs.astype(BF16)
                        score_half = score_grad.astype(BF16)
                        terms = (
                            dot_nn(score_half, query), dot_nn(probs_half, grad),
                            dot_tn(keys, score_half), dot_tn(values, probs_half),
                        )
                        if kb < qb:
                            key_grads[kb] = key_grads[kb] + terms[0]
                            value_grads[kb] = value_grads[kb] + terms[1]
                        else:
                            key_grads[kb] = terms[0]
                            value_grads[kb] = terms[1]
                        query_grad = terms[2] if query_grad is None else query_grad + terms[2]
                        out = terms[3] if out is None else out + terms[3]
                    ab[h, 0, i, rows, :] = (query_grad * SCALE).T.astype(BF16)
                    ab[h, 3, i, rows, :] = out.T.astype(BF16)
                for kb in range(2):
                    where = pl.ds(kb * HALF, HALF)
                    ab[h, 1, i, where, :] = (key_grads[kb] * SCALE).astype(BF16)
                    ab[h, 2, i, where, :] = value_grads[kb].astype(BF16)

            if part == 0:

                def row_src(dst):
                    return ab.at[h, :, pl.ds(0, K), pl.ds(pl.multiple_of(dst * COLS, COLS), COLS)]

                row_dst = row_back.at[h, :, pl.ds(me_c * K, K)]

                @pl.loop(1, NC)
                def _(d):
                    dst = row_peer(d)
                    pltpu.make_async_remote_copy(
                        src_ref=row_src(dst), dst_ref=row_dst, send_sem=out_send.at[0], recv_sem=out_recv.at[0],
                        device_id=(me_r, dst), device_id_type=MESH,
                    ).start()

                pltpu.make_async_copy(row_src(me_c), row_dst, out_recv.at[0]).start()
            else:

                def col_src(dst):
                    return ab.at[h, :, pl.ds(K, K), pl.ds(pl.multiple_of(dst * ROWS, ROWS), ROWS)]

                col_dst = col_back.at[h, :, pl.ds(me_r * K, K)]

                @pl.loop(1, NR)
                def _(d):
                    dst = col_peer(d)
                    pltpu.make_async_remote_copy(
                        src_ref=col_src(dst), dst_ref=col_dst, send_sem=out_send.at[1], recv_sem=out_recv.at[1],
                        device_id=(dst, me_c), device_id_type=MESH,
                    ).start()

                pltpu.make_async_copy(col_src(me_r), col_dst, out_recv.at[1]).start()

    send_in(0)
    send_in(1)

    @pl.loop(0, H + 2)
    def _(t):
        @pl.when(t < H)
        def _():
            forward(t)

        @pl.when(t < H - 2)
        def _():
            send_in(t + 2)

        @pl.when(jnp.logical_and(t >= 1, t <= H))
        def _():
            merge(t - 1)

        @pl.when(t >= 2)
        def _():
            backward(t - 2)

    def drain(ref, sem):
        pltpu.make_async_copy(ref, ref, sem).wait()

    row_sent = ab.at[:, :, pl.ds(0, K), pl.ds(0, G - COLS)]
    col_sent = ab.at[:, :, pl.ds(0, K), pl.ds(0, G - ROWS)]
    drain(row_sent, in_send.at[0])
    drain(col_sent, in_send.at[1])
    drain(row_sent, out_send.at[0])
    drain(col_sent, out_send.at[1])
    drain(rs.at[:, pl.ds(0, NC - 1)], stat_send.at[0])
    drain(cs.at[:, pl.ds(0, NR - 1)], stat_send.at[1])
    drain(rr.at[:, pl.ds(0, NC - 1)], merged_send.at[0])
    drain(cr.at[:, pl.ds(0, NR - 1)], merged_send.at[1])
    drain(row_back, out_recv.at[0])
    drain(col_back, out_recv.at[1])


def add_kernel(row_back, col_back, q_out, k_out, v_out, o_out):
    swap = swap_matrix()
    outs = (q_out, k_out, v_out, o_out)
    for a in range(4):
        for h in range(H):
            first = row_back[h, a].reshape(HALF, E).astype(F32)
            second = dot_nn(swap, col_back[h, a].reshape(HALF, E))
            outs[a][:, :, h * E:(h + 1) * E] = (first + second).astype(BF16).reshape(16, 16, E)


def shards(query_tiles, key_tiles, value_tiles, out_grad):
    any_spec = pl.BlockSpec(memory_space=pl.ANY)
    row_back, col_back = pl.pallas_call(
        kernel,
        out_shape=(
            jax.ShapeDtypeStruct((H, 4, ROWS, COLS, E), BF16),
            jax.ShapeDtypeStruct((H, 4, COLS, ROWS, E), BF16),
        ),
        in_specs=[any_spec] * 4,
        out_specs=(any_spec, any_spec),
        scratch_shapes=[
            pltpu.VMEM((H, 4, ROWS, COLS, E), BF16),
            pltpu.VMEM((H, 4, COLS, ROWS, E), BF16),
            pltpu.VMEM((H, 4, 2 * K, G, E), BF16),
            pltpu.VMEM((HALF, HALF), BF16),
            pltpu.VMEM((G, E), F32),
            pltpu.VMEM((H, 16, G), F32),
            pltpu.VMEM((H, NC, 8, E), F32),
            pltpu.VMEM((H, NR, 8, E), F32),
            pltpu.VMEM((H, NC, 8, E), F32),
            pltpu.VMEM((H, NR, 8, E), F32),
            pltpu.VMEM((H, NC, 8, E), F32),
            pltpu.VMEM((H, NR, 8, E), F32),
            pltpu.VMEM((16, G), F32),
            pltpu.VMEM((2, ROWS, E), F32),
            pltpu.VMEM((2, E, E), F32),
            pltpu.VMEM((2, E, E), F32),
            pltpu.VMEM((2, E, E), F32),
            pltpu.SemaphoreType.DMA((H, 4)),
            pltpu.SemaphoreType.DMA((2,)),
            pltpu.SemaphoreType.DMA((H, 2)),
            pltpu.SemaphoreType.DMA((2,)),
            pltpu.SemaphoreType.DMA((2,)),
            pltpu.SemaphoreType.DMA((2,)),
            pltpu.SemaphoreType.DMA((H, 2)),
            pltpu.SemaphoreType.DMA((2,)),
            pltpu.SemaphoreType.DMA((H, 2)),
        ],
        compiler_params=pltpu.CompilerParams(
            collective_id=0, has_side_effects=True, vmem_limit_bytes=52 * 2**20
        ),
        name="attend",
    )(query_tiles, key_tiles, value_tiles, out_grad)
    out = jax.ShapeDtypeStruct((ROWS, COLS, H * E), BF16)
    query_grad, key_grad, value_grad, attended = pl.pallas_call(
        add_kernel,
        out_shape=(out,) * 4,
        grid=(ROWS // 16, COLS // 16),
        in_specs=[
            pl.BlockSpec((H, 4, 16, 16, E), lambda r, c: (0, 0, r, c, 0)),
            pl.BlockSpec((H, 4, 16, 16, E), lambda r, c: (0, 0, c, r, 0)),
        ],
        out_specs=[pl.BlockSpec((16, 16, H * E), lambda r, c: (r, c, 0))] * 4,
        compiler_params=pltpu.CompilerParams(vmem_limit_bytes=32 * 2**20),
        name="add_parts",
    )(row_back, col_back)
    return attended, query_grad, key_grad, value_grad


def solution(mesh):
    spec = P("row", "col", None)
    return jax.shard_map(
        shards, mesh=mesh, in_specs=(spec,) * 4, out_specs=(spec,) * 4, check_vma=False
    )
```

time: 756 us -> 278 us (0.37); the launches traced: 743 us -> 278 us
  Pallas kernels: 0 us -> 271 us
  local copies, waits for them, and re-layouts: 217 us -> 6.76 us
  waiting for transfers between devices: 164 us -> 0 us
  matrix products: 111 us -> 0 us
  starting transfers between devices: 107 us -> 0 us
  blocking collectives: 92.7 us -> 0 us
  other arithmetic: 49.5 us -> 0 us
    pallas_call x0 -> x2, Pallas kernels: none -> 271 us  [the longest x1 262 us: shards(): pl.pallas_call(kernel, out_shape=(jax.ShapeDtypeStruct((H, 4, ROWS, COLS,...]
    all_to_all x17 -> x0, waiting for transfers between devices: 164 us -> none  [the longest x1 25.3 us: shards(): lax.all_to_all(order_columns(row_side[0], row_count, col_count), ('row',...]
    reshape x28 -> x0, local copies, waits for them, and re-layouts: 112 us -> none  [the longest x14 62.5 us: split_heads(): return array_in.reshape(array_in.shape[:-1] + (H, array_in.shape[-1] // H))]
    dot_general x12 -> x0, matrix products: 111 us -> none  [the longest x2 22.6 us: backward_part(): jnp.einsum(spec_set[2], weights_half, grad_heads, preferred_element_type=...]
    all_to_all x17 -> x0, starting transfers between devices: 107 us -> none  [the longest x1 10.7 us: shards(): lax.all_to_all(order_columns(row_side[2], row_count, col_count), ('row',...]
    all_to_all x3 -> x0, blocking collectives: 92.7 us -> none  [the longest x1 31.3 us: shards(): lax.all_to_all(query_tiles, 'col', split_axis=0, concat_axis=1, tiled=True)]
    all_to_all x23 -> x0, local copies, waits for them, and re-layouts: 58.6 us -> none  [the longest x2 6.53 us: shards(): lax.all_to_all(order_columns(row_dot, row_count, col_count), ('row', 'col...]
    convert_element_type x10 -> x0, other arithmetic: 28 us -> none  [the longest x2 23.6 us: shards(): (row_back[member].astype(jnp.float32) + column_back[member].astype(jnp.fl...]
  transfers between devices with their start and end apart: 17 -> 0, of which waited for: 13 -> 0; matrix products, arithmetic and copies ran while one was open for 45% -> 0% of each run, Pallas kernels for 0% -> 0%
where the time goes in v1:
time: 278 us
  Pallas kernels  271 us (97%)
  local copies, waits for them, and re-layouts  6.76 us (2%)
    pallas_call x1, Pallas kernels, shards(): pl.pallas_call(kernel, out_shape=(jax.ShapeDtypeStruct((H, 4, ROWS, COLS,...  262 us
    pallas_call x1, Pallas kernels, shards(): pl.pallas_call(add_kernel, out_shape=(out,) * 4, grid=(ROWS // 16, COLS /...  8.56 us
    unnamed x4, local copies, waits for them, and re-layouts  6.76 us

profile of v1, /device:TPU:8, one launch (start us, length us, event | category | flops | bytes accessed | tf_op | source)
XLA Modules:
  0.0 278.2 jit_solution(10589508099896956052)
XLA Ops:
  0.6 262.3 %attend.1 = (bf16[4,4,32,64,128]{4,3,2,1,0:T(8,128)(2,1)}, bf16[4,4,64,32,128]{4,3,2,1,0:T(8,128)(2,1)}) custom-call(bf16[32,64,512]{2,1,0:T(8,128)(2,1)} %q_in.1, bf16[32,64,512]{2,1,0:T(8,128)(2,1)} %k_in.1, bf16[32,64,512]{2,1,0:T(8,128)(2,1)} %v_in.1, bf16[32,64,512]{2,1,0:T(8,128)(2,1)} %g_in.1), custom_call_target="tpu_custom_call" | custom-call | tf_op jit(solution)/shard_map/attend/pallas_call | solution.py:395
  262.9 0.0 copy-start
  262.9 3.4 %copy-done = bf16[4,4,32,64,128]{4,3,2,1,0:T(8,128)(2,1)S(1)} copy-done((bf16[4,4,32,64,128]{4,3,2,1,0:T(8,128)(2,1)S(1)}, bf16[4,4,32,64,128]{4,3,2,1,0:T(8,128)(2,1)}, u32[]{:S(2)}) %copy-start) | copy-done | bytes 8388632
  266.3 0.0 copy-start.1
  266.3 3.4 %copy-done.1 = bf16[4,4,64,32,128]{4,3,2,1,0:T(8,128)(2,1)S(1)} copy-done((bf16[4,4,64,32,128]{4,3,2,1,0:T(8,128)(2,1)S(1)}, bf16[4,4,64,32,128]{4,3,2,1,0:T(8,128)(2,1)}, u32[]{:S(2)}) %copy-start.1) | copy-done | bytes 8388632
  269.7 8.6 %add_parts.1 = (bf16[32,64,512]{2,1,0:T(8,128)(2,1)}, bf16[32,64,512]{2,1,0:T(8,128)(2,1)}, bf16[32,64,512]{2,1,0:T(8,128)(2,1)}, bf16[32,64,512]{2,1,0:T(8,128)(2,1)}) custom-call(bf16[4,4,32,64,128]{4,3,2,1,0:T(8,128)(2,1)S(1)} %copy-done, bf16[4,4,64,32,128]{4,3,2,1,0:T(8,128)(2,1)S(1)} %copy-done.1), custom_call_target="tpu_custom_call" | custom-call | tf_op jit(solution)/shard_map/add_parts/pallas_call | solution.py:437
Async XLA Ops:
  262.9 3.4 %copy-start = (bf16[4,4,32,64,128]{4,3,2,1,0:T(8,128)(2,1)S(1)}, bf16[4,4,32,64,128]{4,3,2,1,0:T(8,128)(2,1)}, u32[]{:S(2)}) copy-start(bf16[4,4,32,64,128]{4,3,2,1,0:T(8,128)(2,1)} %get-tuple-element.10.row_back) | copy-start | bytes 25165828
  266.3 3.4 %copy-start.1 = (bf16[4,4,64,32,128]{4,3,2,1,0:T(8,128)(2,1)S(1)}, bf16[4,4,64,32,128]{4,3,2,1,0:T(8,128)(2,1)}, u32[]{:S(2)}) copy-start(bf16[4,4,64,32,128]{4,3,2,1,0:T(8,128)(2,1)} %get-tuple-element.11.col_back) | copy-start | bytes 25165828

commit v2 on v1

--- a/solution.py
+++ b/solution.py
@@ -114,20 +114,20 @@
                     moved = dot_nn(perm[...], block.reshape(HALF, E)).astype(BF16)
                     xt[h, a, cb * 16:cb * 16 + 16, rb * 16:rb * 16 + 16, :] = moved.reshape(16, 16, E)
 
-        def col_src(dst):
-            return xt.at[h, :, pl.ds(dst * K, K)]
-
-        col_dst = ab.at[h, :, pl.ds(K, K), pl.ds(pl.multiple_of(me_r * ROWS, ROWS), ROWS)]
-
-        @pl.loop(1, NR)
-        def _(d):
-            dst = col_peer(d)
-            pltpu.make_async_remote_copy(
-                src_ref=col_src(dst), dst_ref=col_dst, send_sem=in_send.at[1], recv_sem=in_recv.at[h, 1],
-                device_id=(dst, me_c), device_id_type=MESH,
-            ).start()
-
-        pltpu.make_async_copy(col_src(me_r), col_dst, in_recv.at[h, 1]).start()
+            def col_src(dst):
+                return xt.at[h, a, pl.ds(dst * K, K)]
+
+            col_dst = ab.at[h, a, pl.ds(K, K), pl.ds(pl.multiple_of(me_r * ROWS, ROWS), ROWS)]
+
+            @pl.loop(1, NR)
+            def _(d):
+                dst = col_peer(d)
+                pltpu.make_async_remote_copy(
+                    src_ref=col_src(dst), dst_ref=col_dst, send_sem=in_send.at[1], recv_sem=in_recv.at[h, 1],
+                    device_id=(dst, me_c), device_id_type=MESH,
+                ).start()
+
+            pltpu.make_async_copy(col_src(me_r), col_dst, in_recv.at[h, 1]).start()
 
     def forward(h):
         lane = lax.broadcasted_iota(jnp.int32, (HALF, E), 1)
@@ -327,20 +327,22 @@
                 pltpu.make_async_copy(row_src(me_c), row_dst, out_recv.at[0]).start()
             else:
 
-                def col_src(dst):
-                    return ab.at[h, :, pl.ds(K, K), pl.ds(pl.multiple_of(dst * ROWS, ROWS), ROWS)]
-
-                col_dst = col_back.at[h, :, pl.ds(me_r * K, K)]
-
-                @pl.loop(1, NR)
-                def _(d):
-                    dst = col_peer(d)
-                    pltpu.make_async_remote_copy(
-                        src_ref=col_src(dst), dst_ref=col_dst, send_sem=out_send.at[1], recv_sem=out_recv.at[1],
-                        device_id=(dst, me_c), device_id_type=MESH,
-                    ).start()
-
-                pltpu.make_async_copy(col_src(me_r), col_dst, out_recv.at[1]).start()
+                @pl.loop(0, 4)
+                def _(a):
+                    def col_src(dst):
+                        return ab.at[h, a, pl.ds(K, K), pl.ds(pl.multiple_of(dst * ROWS, ROWS), ROWS)]
+
+                    col_dst = col_back.at[h, a, pl.ds(me_r * K, K)]
+
+                    @pl.loop(1, NR)
+                    def _(d):
+                        dst = col_peer(d)
+                        pltpu.make_async_remote_copy(
+                            src_ref=col_src(dst), dst_ref=col_dst, send_sem=out_send.at[1],
+                            recv_sem=out_recv.at[1], device_id=(dst, me_c), device_id_type=MESH,
+                        ).start()
+
+                    pltpu.make_async_copy(col_src(me_r), col_dst, out_recv.at[1]).start()
 
     send_in(0)
     send_in(1)
@@ -443,7 +445,7 @@
             pl.BlockSpec((H, 4, 16, 16, E), lambda r, c: (0, 0, c, r, 0)),
         ],
         out_specs=[pl.BlockSpec((16, 16, H * E), lambda r, c: (r, c, 0))] * 4,
-        compiler_params=pltpu.CompilerParams(vmem_limit_bytes=32 * 2**20),
+        compiler_params=pltpu.CompilerParams(vmem_limit_bytes=60 * 2**20),
         name="add_parts",
     )(row_back, col_back)
     return attended, query_grad, key_grad, value_grad

time: 278 us -> 222 us (0.80)
  Pallas kernels: 271 us -> 220 us
  local copies, waits for them, and re-layouts: 6.76 us -> 0 us
    pallas_call x1, Pallas kernels: 262 us -> 207 us  [shards(): pl.pallas_call(kernel, out_shape=(jax.ShapeDtypeStruct((H, 4, ROWS, COLS,...]
    unnamed x4 -> x0, local copies, waits for them, and re-layouts: 6.76 us -> none
    pallas_call x1, Pallas kernels: 8.56 us -> 13.1 us  [shards(): pl.pallas_call(add_kernel, out_shape=(out,) * 4, grid=(ROWS // 16, COLS /...]
where the time goes in v2:
time: 222 us; the launch traced here: 221 us
  Pallas kernels  220 us (99%)
    pallas_call x1, Pallas kernels, shards(): pl.pallas_call(kernel, out_shape=(jax.ShapeDtypeStruct((H, 4, ROWS, COLS,...  207 us
    pallas_call x1, Pallas kernels, shards(): pl.pallas_call(add_kernel, out_shape=(out,) * 4, grid=(ROWS // 16, COLS /...  13.1 us

profile of v2, /device:TPU:8, one launch (start us, length us, event | category | flops | bytes accessed | tf_op | source)
XLA Modules:
  0.0 220.9 jit_solution(15698388407688849579)
XLA Ops:
  0.6 207.2 %attend.1 = (bf16[4,4,32,64,128]{4,3,2,1,0:T(8,128)(2,1)}, bf16[4,4,64,32,128]{4,3,2,1,0:T(8,128)(2,1)}) custom-call(bf16[32,64,512]{2,1,0:T(8,128)(2,1)} %q_in.1, bf16[32,64,512]{2,1,0:T(8,128)(2,1)} %k_in.1, bf16[32,64,512]{2,1,0:T(8,128)(2,1)} %v_in.1, bf16[32,64,512]{2,1,0:T(8,128)(2,1)} %g_in.1), custom_call_target="tpu_custom_call" | custom-call | tf_op jit(solution)/shard_map/attend/pallas_call | solution.py:397
  207.8 13.1 %add_parts.1 = (bf16[32,64,512]{2,1,0:T(8,128)(2,1)}, bf16[32,64,512]{2,1,0:T(8,128)(2,1)}, bf16[32,64,512]{2,1,0:T(8,128)(2,1)}, bf16[32,64,512]{2,1,0:T(8,128)(2,1)}) custom-call(bf16[4,4,32,64,128]{4,3,2,1,0:T(8,128)(2,1)} %get-tuple-element.10.row_back, bf16[4,4,64,32,128]{4,3,2,1,0:T(8,128)(2,1)} %get-tuple-element.11.col_back), custom_call_target="tpu_custom_call" | custom-call | tf_op jit(solution)/shard_map/add_parts/pallas_call | solution.py:439

commit v3 on v2

--- a/solution.py
+++ b/solution.py
@@ -19,6 +19,7 @@
 LOG2E = 1.4426950408889634
 SCALE = E ** (-0.5)
 NEG = -1e30
+MOVES = 2
 MESH = pl.DeviceIdType.MESH
 F32 = jnp.float32
 BF16 = jnp.bfloat16
@@ -44,9 +45,10 @@
 
 
 def kernel(
-    q_in, k_in, v_in, g_in, row_back, col_back,
+    q_in, k_in, v_in, g_in, row_back, col_back, q_sum, k_sum, v_sum, o_sum,
     xs, xt, ab, perm, st, so, rs, cs, mr, mc, rr, cr, mm, pr, pc, ct, lt,
     load_sem, in_send, in_recv, out_send, out_recv, stat_send, stat_recv, merged_send, merged_recv,
+    back_sem, sum_sem,
 ):
     me_r = lax.axis_index("row")
     me_c = lax.axis_index("col")
@@ -68,9 +70,8 @@
             for a in range(4)
         ]
 
-    for h in range(H):
-        for copy in load(h):
-            copy.start()
+    for copy in load(0):
+        copy.start()
 
     barrier = pltpu.get_barrier_semaphore()
 
@@ -90,6 +91,11 @@
     def send_in(h):
         for copy in load(h):
             copy.wait()
+
+        @pl.when(h < H - 1)
+        def _():
+            for copy in load(h + 1):
+                copy.start()
 
         def row_src(dst):
             return xs.at[h, :, pl.ds(dst * K, K)]
@@ -264,85 +270,82 @@
         k_pos = lax.broadcasted_iota(jnp.int32, (HALF, HALF), 0)
         q_pos = lax.broadcasted_iota(jnp.int32, (HALF, HALF), 1)
 
-        for part in range(2):
-
-            @pl.loop(0, K)
-            def _(k):
-                i = part * K + k
-                allowed = k_pos <= q_pos - part
-                key_grads = [None, None]
-                value_grads = [None, None]
-                for qb in range(2):
-                    rows = pl.ds(qb * HALF, HALF)
-                    query = ab[h, 0, i, rows, :]
-                    grad = ab[h, 3, i, rows, :]
-                    log_total = mm[pl.ds(part * 8 + k, 1), rows]
-                    delta = mm[pl.ds(part * 8 + 4 + k, 1), rows]
-                    query_grad = None
-                    out = None
-                    for kb in range(qb + 1):
-                        keys = ab[h, 1, i, pl.ds(kb * HALF, HALF), :]
-                        values = ab[h, 2, i, pl.ds(kb * HALF, HALF), :]
-                        scores = dot_nt(keys, query) * (SCALE * LOG2E)
-                        if kb == qb:
-                            scores = jnp.where(allowed, scores, NEG)
-                        probs = jnp.exp2(scores - log_total)
-                        score_grad = probs * (dot_nt(values, grad) - delta)
-                        probs_half = probs.astype(BF16)
-                        score_half = score_grad.astype(BF16)
-                        terms = (
-                            dot_nn(score_half, query), dot_nn(probs_half, grad),
-                            dot_tn(keys, score_half), dot_tn(values, probs_half),
-                        )
-                        if kb < qb:
-                            key_grads[kb] = key_grads[kb] + terms[0]
-                            value_grads[kb] = value_grads[kb] + terms[1]
-                        else:
-                            key_grads[kb] = terms[0]
-                            value_grads[kb] = terms[1]
-                        query_grad = terms[2] if query_grad is None else query_grad + terms[2]
-                        out = terms[3] if out is None else out + terms[3]
-                    ab[h, 0, i, rows, :] = (query_grad * SCALE).T.astype(BF16)
-                    ab[h, 3, i, rows, :] = out.T.astype(BF16)
-                for kb in range(2):
-                    where = pl.ds(kb * HALF, HALF)
-                    ab[h, 1, i, where, :] = (key_grads[kb] * SCALE).astype(BF16)
-                    ab[h, 2, i, where, :] = value_grads[kb].astype(BF16)
-
-            if part == 0:
-
-                def row_src(dst):
-                    return ab.at[h, :, pl.ds(0, K), pl.ds(pl.multiple_of(dst * COLS, COLS), COLS)]
-
-                row_dst = row_back.at[h, :, pl.ds(me_c * K, K)]
-
-                @pl.loop(1, NC)
-                def _(d):
-                    dst = row_peer(d)
-                    pltpu.make_async_remote_copy(
-                        src_ref=row_src(dst), dst_ref=row_dst, send_sem=out_send.at[0], recv_sem=out_recv.at[0],
-                        device_id=(me_r, dst), device_id_type=MESH,
-                    ).start()
-
-                pltpu.make_async_copy(row_src(me_c), row_dst, out_recv.at[0]).start()
-            else:
-
-                @pl.loop(0, 4)
-                def _(a):
-                    def col_src(dst):
-                        return ab.at[h, a, pl.ds(K, K), pl.ds(pl.multiple_of(dst * ROWS, ROWS), ROWS)]
-
-                    col_dst = col_back.at[h, a, pl.ds(me_r * K, K)]
-
-                    @pl.loop(1, NR)
-                    def _(d):
-                        dst = col_peer(d)
-                        pltpu.make_async_remote_copy(
-                            src_ref=col_src(dst), dst_ref=col_dst, send_sem=out_send.at[1],
-                            recv_sem=out_recv.at[1], device_id=(dst, me_c), device_id_type=MESH,
-                        ).start()
-
-                    pltpu.make_async_copy(col_src(me_r), col_dst, out_recv.at[1]).start()
+        def instance(part, k):
+            i = part * K + k
+            allowed = k_pos <= q_pos - part
+            key_grads = [None, None]
+            value_grads = [None, None]
+            for qb in range(2):
+                rows = pl.ds(qb * HALF, HALF)
+                query = ab[h, 0, i, rows, :]
+                grad = ab[h, 3, i, rows, :]
+                log_total = mm[pl.ds(part * 8 + k, 1), rows]
+                delta = mm[pl.ds(part * 8 + 4 + k, 1), rows]
+                query_grad = None
+                out = None
+                for kb in range(qb + 1):
+                    keys = ab[h, 1, i, pl.ds(kb * HALF, HALF), :]
+                    values = ab[h, 2, i, pl.ds(kb * HALF, HALF), :]
+                    scores = dot_nt(keys, query) * (SCALE * LOG2E)
+                    if kb == qb:
+                        scores = jnp.where(allowed, scores, NEG)
+                    probs = jnp.exp2(scores - log_total)
+                    score_grad = probs * (dot_nt(values, grad) - delta)
+                    probs_half = probs.astype(BF16)
+                    score_half = score_grad.astype(BF16)
+                    terms = (
+                        dot_nn(score_half, query), dot_nn(probs_half, grad),
+                        dot_tn(keys, score_half), dot_tn(values, probs_half),
+                    )
+                    if kb < qb:
+                        key_grads[kb] = key_grads[kb] + terms[0]
+                        value_grads[kb] = value_grads[kb] + terms[1]
+                    else:
+                        key_grads[kb] = terms[0]
+                        value_grads[kb] = terms[1]
+                    query_grad = terms[2] if query_grad is None else query_grad + terms[2]
+                    out = terms[3] if out is None else out + terms[3]
+                ab[h, 0, i, rows, :] = (query_grad * SCALE).T.astype(BF16)
+                ab[h, 3, i, rows, :] = out.T.astype(BF16)
+            for kb in range(2):
+                where = pl.ds(kb * HALF, HALF)
+                ab[h, 1, i, where, :] = (key_grads[kb] * SCALE).astype(BF16)
+                ab[h, 2, i, where, :] = value_grads[kb].astype(BF16)
+
+        @pl.loop(0, K)
+        def _(k):
+            instance(0, k)
+
+            def row_src(dst):
+                return ab.at[h, :, k, pl.ds(pl.multiple_of(dst * COLS, COLS), COLS)]
+
+            row_dst = row_back.at[h, :, me_c * K + k]
+
+            @pl.loop(1, NC)
+            def _(d):
+                dst = row_peer(d)
+                pltpu.make_async_remote_copy(
+                    src_ref=row_src(dst), dst_ref=row_dst, send_sem=out_send.at[0],
+                    recv_sem=out_recv.at[h, 0], device_id=(me_r, dst), device_id_type=MESH,
+                ).start()
+
+            pltpu.make_async_copy(row_src(me_c), row_dst, out_recv.at[h, 0]).start()
+            instance(1, k)
+
+            def col_src(dst):
+                return ab.at[h, :, K + k, pl.ds(pl.multiple_of(dst * ROWS, ROWS), ROWS)]
+
+            col_dst = col_back.at[h, :, me_r * K + k]
+
+            @pl.loop(1, NR)
+            def _(d):
+                dst = col_peer(d)
+                pltpu.make_async_remote_copy(
+                    src_ref=col_src(dst), dst_ref=col_dst, send_sem=out_send.at[1],
+                    recv_sem=out_recv.at[h, 1], device_id=(dst, me_c), device_id_type=MESH,
+                ).start()
+
+            pltpu.make_async_copy(col_src(me_r), col_dst, out_recv.at[h, 1]).start()
 
     send_in(0)
     send_in(1)
@@ -372,36 +375,110 @@
     col_sent = ab.at[:, :, pl.ds(0, K), pl.ds(0, G - ROWS)]
     drain(row_sent, in_send.at[0])
     drain(col_sent, in_send.at[1])
+
+    sums = (q_sum, k_sum, v_sum, o_sum)
+
+    def store(h, a):
+        return pltpu.make_async_copy(xs.at[h, a], sums[a].at[:, :, h * E:(h + 1) * E], sum_sem.at[h, a])
+
+    for h in range(H - 1):
+        drain(row_back.at[h], out_recv.at[h, 0])
+        drain(col_back.at[h], out_recv.at[h, 1])
+        backs = [
+            pltpu.make_async_copy(row_back.at[h], xs.at[h], back_sem.at[h, 0]),
+            pltpu.make_async_copy(col_back.at[h], xt.at[h], back_sem.at[h, 1]),
+        ]
+        for copy in backs:
+            copy.start()
+        for copy in backs:
+            copy.wait()
+
+        @pl.loop(0, COLS // 16)
+        def _(cb):
+            add_block(perm, xs.at[h], xt.at[h], xs.at[h], cb)
+
+        for a in range(4):
+            store(h, a).start()
+
+    for h in range(H - 1):
+        for a in range(4):
+            store(h, a).wait()
     drain(row_sent, out_send.at[0])
     drain(col_sent, out_send.at[1])
     drain(rs.at[:, pl.ds(0, NC - 1)], stat_send.at[0])
     drain(cs.at[:, pl.ds(0, NR - 1)], stat_send.at[1])
     drain(rr.at[:, pl.ds(0, NC - 1)], merged_send.at[0])
     drain(cr.at[:, pl.ds(0, NR - 1)], merged_send.at[1])
-    drain(row_back, out_recv.at[0])
-    drain(col_back, out_recv.at[1])
-
-
-def add_kernel(row_back, col_back, q_out, k_out, v_out, o_out):
-    swap = swap_matrix()
+    drain(row_back.at[H - 1], out_recv.at[H - 1, 0])
+    drain(col_back.at[H - 1], out_recv.at[H - 1, 1])
+
+
+def add_block(perm, first, second, total, cb):
+    cols = pl.ds(cb * 16 if isinstance(cb, int) else pl.multiple_of(cb * 16, 16), 16)
+    for rb in range(ROWS // 16):
+        rows = pl.ds(rb * 16, 16)
+        for a in range(0, 4, 2):
+            pair = [second[a + n, cols, rows, :].reshape(HALF, E) for n in range(2)]
+            moved = dot_nn(perm[...], jnp.concatenate(pair, axis=1))
+            for n in range(2):
+                mine = first[a + n, rows, cols, :].reshape(HALF, E).astype(F32)
+                both = (mine + moved[:, n * E:(n + 1) * E]).astype(BF16)
+                total[a + n, rows, cols, :] = both.reshape(16, 16, E)
+
+
+def add_kernel(
+    row_back, col_back, q_sum, k_sum, v_sum, o_sum, q_out, k_out, v_out, o_out,
+    first, second, stage, perm, back_sem, out_sem, load_sem, store_sem,
+):
+    sums = (q_sum, k_sum, v_sum, o_sum)
     outs = (q_out, k_out, v_out, o_out)
-    for a in range(4):
-        for h in range(H):
-            first = row_back[h, a].reshape(HALF, E).astype(F32)
-            second = dot_nn(swap, col_back[h, a].reshape(HALF, E))
-            outs[a][:, :, h * E:(h + 1) * E] = (first + second).astype(BF16).reshape(16, 16, E)
+    backs = [
+        pltpu.make_async_copy(row_back.at[H - 1], first, back_sem.at[0]),
+        pltpu.make_async_copy(col_back.at[H - 1], second, back_sem.at[1]),
+    ]
+    for copy in backs:
+        copy.start()
+    loads = []
+    stores = []
+    for n in range(MOVES):
+        for a in range(4):
+            part = (pl.ds(n * (ROWS // MOVES), ROWS // MOVES), slice(None), pl.ds(0, (H - 1) * E))
+            here = stage.at[(a,) + part[:2]]
+            loads.append(pltpu.make_async_copy(sums[a].at[part], here, load_sem.at[a, n]))
+            stores.append(pltpu.make_async_copy(here, outs[a].at[part], store_sem.at[a, n]))
+    for copy in loads:
+        copy.start()
+    perm[...] = swap_matrix()
+    for copy in backs:
+        copy.wait()
+    step = len(loads) // (COLS // 16)
+    for cb in range(COLS // 16):
+        add_block(perm, first, second, first, cb)
+        for n in range(cb * step, cb * step + step):
+            loads[n].wait()
+            stores[n].start()
+    last = [
+        pltpu.make_async_copy(first.at[a], outs[a].at[:, :, pl.ds((H - 1) * E, E)], out_sem.at[a])
+        for a in range(4)
+    ]
+    for copy in last:
+        copy.start()
+    for copy in last + stores:
+        copy.wait()
 
 
 def shards(query_tiles, key_tiles, value_tiles, out_grad):
     any_spec = pl.BlockSpec(memory_space=pl.ANY)
-    row_back, col_back = pl.pallas_call(
+    out = jax.ShapeDtypeStruct((ROWS, COLS, H * E), BF16)
+    backs = (
+        jax.ShapeDtypeStruct((H, 4, ROWS, COLS, E), BF16),
+        jax.ShapeDtypeStruct((H, 4, COLS, ROWS, E), BF16),
+    )
+    returned = pl.pallas_call(
         kernel,
-        out_shape=(
-            jax.ShapeDtypeStruct((H, 4, ROWS, COLS, E), BF16),
-            jax.ShapeDtypeStruct((H, 4, COLS, ROWS, E), BF16),
-        ),
+        out_shape=backs + (out,) * 4,
         in_specs=[any_spec] * 4,
-        out_specs=(any_spec, any_spec),
+        out_specs=(any_spec,) * 6,
         scratch_shapes=[
             pltpu.VMEM((H, 4, ROWS, COLS, E), BF16),
             pltpu.VMEM((H, 4, COLS, ROWS, E), BF16),
@@ -424,30 +501,37 @@
             pltpu.SemaphoreType.DMA((2,)),
             pltpu.SemaphoreType.DMA((H, 2)),
             pltpu.SemaphoreType.DMA((2,)),
-            pltpu.SemaphoreType.DMA((2,)),
+            pltpu.SemaphoreType.DMA((H, 2)),
             pltpu.SemaphoreType.DMA((2,)),
             pltpu.SemaphoreType.DMA((H, 2)),
             pltpu.SemaphoreType.DMA((2,)),
             pltpu.SemaphoreType.DMA((H, 2)),
+            pltpu.SemaphoreType.DMA((H, 2)),
+            pltpu.SemaphoreType.DMA((H, 4)),
         ],
         compiler_params=pltpu.CompilerParams(
             collective_id=0, has_side_effects=True, vmem_limit_bytes=52 * 2**20
         ),
         name="attend",
     )(query_tiles, key_tiles, value_tiles, out_grad)
-    out = jax.ShapeDtypeStruct((ROWS, COLS, H * E), BF16)
     query_grad, key_grad, value_grad, attended = pl.pallas_call(
         add_kernel,
         out_shape=(out,) * 4,
-        grid=(ROWS // 16, COLS // 16),
-        in_specs=[
-            pl.BlockSpec((H, 4, 16, 16, E), lambda r, c: (0, 0, r, c, 0)),
-            pl.BlockSpec((H, 4, 16, 16, E), lambda r, c: (0, 0, c, r, 0)),
+        in_specs=[any_spec] * 6,
+        out_specs=(any_spec,) * 4,
+        scratch_shapes=[
+            pltpu.VMEM((4, ROWS, COLS, E), BF16),
+            pltpu.VMEM((4, COLS, ROWS, E), BF16),
+            pltpu.VMEM((4, ROWS, COLS, (H - 1) * E), BF16),
+            pltpu.VMEM((HALF, HALF), BF16),
+            pltpu.SemaphoreType.DMA((2,)),
+            pltpu.SemaphoreType.DMA((4,)),
+            pltpu.SemaphoreType.DMA((4, MOVES)),
+            pltpu.SemaphoreType.DMA((4, MOVES)),
         ],
-        out_specs=[pl.BlockSpec((16, 16, H * E), lambda r, c: (r, c, 0))] * 4,
         compiler_params=pltpu.CompilerParams(vmem_limit_bytes=60 * 2**20),
         name="add_parts",
-    )(row_back, col_back)
+    )(*returned)
     return attended, query_grad, key_grad, value_grad
 
 

time: 222 us -> 212 us (0.955)
  Pallas kernels: 220 us -> 211 us
    pallas_call x2, Pallas kernels: 220 us -> 211 us  [the longest x1 203 us: shards(): pl.pallas_call(kernel, out_shape=backs + (out,) * 4, in_specs=[any_spec]...]
where the time goes in v3:
time: 212 us; the launch traced here: 211 us
  Pallas kernels  211 us (100%)
    pallas_call x1, Pallas kernels, shards(): pl.pallas_call(kernel, out_shape=backs + (out,) * 4, in_specs=[any_spec]...  203 us
    pallas_call x1, Pallas kernels, shards(): pl.pallas_call(add_kernel, out_shape=(out,) * 4, in_specs=[any_spec] * 6,...  7.66 us

profile of v3, /device:TPU:8, one launch (start us, length us, event | category | flops | bytes accessed | tf_op | source)
XLA Modules:
  0.0 211.5 jit_solution(7684853572918577794)
XLA Ops:
  0.6 203.2 %attend.1 = (bf16[4,4,32,64,128]{4,3,2,1,0:T(8,128)(2,1)}, bf16[4,4,64,32,128]{4,3,2,1,0:T(8,128)(2,1)}, bf16[32,64,512]{2,1,0:T(8,128)(2,1)}, bf16[32,64,512]{2...) custom-call(bf16[32,64,512]{2,1,0:T(8,128)(2,1)} %q_in.1, bf16[32,64,512]{2,1,0:T(8,128)(2,1)} %k_in.1, ...), custom_call_target="tpu_custom_call" | custom-call | tf_op jit(solution)/shard_map/attend/pallas_call | solution.py:477
  203.8 7.7 %add_parts.1 = (bf16[32,64,512]{2,1,0:T(8,128)(2,1)}, bf16[32,64,512]{2,1,0:T(8,128)(2,1)}, bf16[32,64,512]{2,1,0:T(8,128)(2,1)}, bf16[32,64,512]{2,1,0:T(8,128)(2,1)}) custom-call(bf16[4,4,32,64,128]{4,3,2,1,0:T(8,128)(2,1)} %get-tuple-element.14.row_back, bf16[4,4,64,32,128]{4,3,2,1,0:T(8,128)(2,1)} %get-tuple-element.15.col_back, ...), custom_call_target="tpu_custom_call" | custom-call | tf_op jit(solution)/shard_map/add_parts/pallas_call | solution.py:517

commit v4 on v3

--- a/solution.py
+++ b/solution.py
@@ -70,6 +70,13 @@
             for a in range(4)
         ]
 
+    def turn(h, a):
+        for cb in range(COLS // 16):
+            for rb in range(ROWS // 16):
+                block = xs[h, a, rb * 16:rb * 16 + 16, cb * 16:cb * 16 + 16, :]
+                moved = dot_nn(perm[...], block.reshape(HALF, E)).astype(BF16)
+                xt[h, a, cb * 16:cb * 16 + 16, rb * 16:rb * 16 + 16, :] = moved.reshape(16, 16, E)
+
     for copy in load(0):
         copy.start()
 
@@ -86,11 +93,16 @@
     perm[...] = swap_matrix()
     st[...] = jnp.zeros_like(st)
     lt[...] = jnp.zeros_like(lt)
+    for copy in load(0):
+        copy.wait()
+    turn(0, 0)
     pl.semaphore_wait(barrier, NC + NR - 2)
 
     def send_in(h):
-        for copy in load(h):
-            copy.wait()
+        @pl.when(h > 0)
+        def _():
+            for copy in load(h):
+                copy.wait()
 
         @pl.when(h < H - 1)
         def _():
@@ -114,11 +126,9 @@
 
         @pl.loop(0, 4)
         def _(a):
-            for cb in range(COLS // 16):
-                for rb in range(ROWS // 16):
-                    block = xs[h, a, rb * 16:rb * 16 + 16, cb * 16:cb * 16 + 16, :]
-                    moved = dot_nn(perm[...], block.reshape(HALF, E)).astype(BF16)
-                    xt[h, a, cb * 16:cb * 16 + 16, rb * 16:rb * 16 + 16, :] = moved.reshape(16, 16, E)
+            @pl.when(h + a > 0)
+            def _():
+                turn(h, a)
 
             def col_src(dst):
                 return xt.at[h, a, pl.ds(dst * K, K)]
@@ -314,6 +324,22 @@
 
         @pl.loop(0, K)
         def _(k):
+            instance(1, k)
+
+            def col_src(dst):
+                return ab.at[h, :, K + k, pl.ds(pl.multiple_of(dst * ROWS, ROWS), ROWS)]
+
+            col_dst = col_back.at[h, :, me_r * K + k]
+
+            @pl.loop(1, NR)
+            def _(d):
+                dst = col_peer(d)
+                pltpu.make_async_remote_copy(
+                    src_ref=col_src(dst), dst_ref=col_dst, send_sem=out_send.at[1],
+                    recv_sem=out_recv.at[h, 1], device_id=(dst, me_c), device_id_type=MESH,
+                ).start()
+
+            pltpu.make_async_copy(col_src(me_r), col_dst, out_recv.at[h, 1]).start()
             instance(0, k)
 
             def row_src(dst):
@@ -330,22 +356,6 @@
                 ).start()
 
             pltpu.make_async_copy(row_src(me_c), row_dst, out_recv.at[h, 0]).start()
-            instance(1, k)
-
-            def col_src(dst):
-                return ab.at[h, :, K + k, pl.ds(pl.multiple_of(dst * ROWS, ROWS), ROWS)]
-
-            col_dst = col_back.at[h, :, me_r * K + k]
-
-            @pl.loop(1, NR)
-            def _(d):
-                dst = col_peer(d)
-                pltpu.make_async_remote_copy(
-                    src_ref=col_src(dst), dst_ref=col_dst, send_sem=out_send.at[1],
-                    recv_sem=out_recv.at[h, 1], device_id=(dst, me_c), device_id_type=MESH,
-                ).start()
-
-            pltpu.make_async_copy(col_src(me_r), col_dst, out_recv.at[h, 1]).start()
 
     send_in(0)
     send_in(1)

time: 212 us -> 210 us (level)
  no operation moved by 1% of the time
where the time goes in v4:
time: 210 us
  Pallas kernels  209 us (100%)
    pallas_call x1, Pallas kernels, shards(): pl.pallas_call(kernel, out_shape=backs + (out,) * 4, in_specs=[any_spec]...  202 us
    pallas_call x1, Pallas kernels, shards(): pl.pallas_call(add_kernel, out_shape=(out,) * 4, in_specs=[any_spec] * 6,...  7.66 us

profile of v4, /device:TPU:8, one launch (start us, length us, event | category | flops | bytes accessed | tf_op | source)
XLA Modules:
  0.0 209.9 jit_solution(5105801563226978760)
XLA Ops:
  0.6 201.7 %attend.1 = (bf16[4,4,32,64,128]{4,3,2,1,0:T(8,128)(2,1)}, bf16[4,4,64,32,128]{4,3,2,1,0:T(8,128)(2,1)}, bf16[32,64,512]{2,1,0:T(8,128)(2,1)}, bf16[32,64,512]{2...) custom-call(bf16[32,64,512]{2,1,0:T(8,128)(2,1)} %q_in.1, bf16[32,64,512]{2,1,0:T(8,128)(2,1)} %k_in.1, ...), custom_call_target="tpu_custom_call" | custom-call | tf_op jit(solution)/shard_map/attend/pallas_call | solution.py:487
  202.3 7.7 %add_parts.1 = (bf16[32,64,512]{2,1,0:T(8,128)(2,1)}, bf16[32,64,512]{2,1,0:T(8,128)(2,1)}, bf16[32,64,512]{2,1,0:T(8,128)(2,1)}, bf16[32,64,512]{2,1,0:T(8,128)(2,1)}) custom-call(bf16[4,4,32,64,128]{4,3,2,1,0:T(8,128)(2,1)} %get-tuple-element.14.row_back, bf16[4,4,64,32,128]{4,3,2,1,0:T(8,128)(2,1)} %get-tuple-element.15.col_back, ...), custom_call_target="tpu_custom_call" | custom-call | tf_op jit(solution)/shard_map/add_parts/pallas_call | solution.py:527

commit v5 on v4

--- a/solution.py
+++ b/solution.py
@@ -19,7 +19,7 @@
 LOG2E = 1.4426950408889634
 SCALE = E ** (-0.5)
 NEG = -1e30
-MOVES = 2
+MOVES = 1
 MESH = pl.DeviceIdType.MESH
 F32 = jnp.float32
 BF16 = jnp.bfloat16
@@ -114,16 +114,6 @@
 
         row_dst = ab.at[h, :, pl.ds(0, K), pl.ds(pl.multiple_of(me_c * COLS, COLS), COLS)]
 
-        @pl.loop(1, NC)
-        def _(d):
-            dst = row_peer(d)
-            pltpu.make_async_remote_copy(
-                src_ref=row_src(dst), dst_ref=row_dst, send_sem=in_send.at[0], recv_sem=in_recv.at[h, 0],
-                device_id=(me_r, dst), device_id_type=MESH,
-            ).start()
-
-        pltpu.make_async_copy(row_src(me_c), row_dst, in_recv.at[h, 0]).start()
-
         @pl.loop(0, 4)
         def _(a):
             @pl.when(h + a > 0)
@@ -144,6 +134,18 @@
                 ).start()
 
             pltpu.make_async_copy(col_src(me_r), col_dst, in_recv.at[h, 1]).start()
+
+            @pl.when(a == 0)
+            def _():
+                @pl.loop(1, NC)
+                def _(d):
+                    dst = row_peer(d)
+                    pltpu.make_async_remote_copy(
+                        src_ref=row_src(dst), dst_ref=row_dst, send_sem=in_send.at[0], recv_sem=in_recv.at[h, 0],
+                        device_id=(me_r, dst), device_id_type=MESH,
+                    ).start()
+
+                pltpu.make_async_copy(row_src(me_c), row_dst, in_recv.at[h, 0]).start()
 
     def forward(h):
         lane = lax.broadcasted_iota(jnp.int32, (HALF, E), 1)

time: 210 us -> 209 us (level)
  no operation moved by 1% of the time
where the time goes in v5:
time: 209 us
  Pallas kernels  208 us (100%)
    pallas_call x1, Pallas kernels, shards(): pl.pallas_call(kernel, out_shape=backs + (out,) * 4, in_specs=[any_spec]...  201 us
    pallas_call x1, Pallas kernels, shards(): pl.pallas_call(add_kernel, out_shape=(out,) * 4, in_specs=[any_spec] * 6,...  7.35 us

profile of v5, /device:TPU:8, one launch (start us, length us, event | category | flops | bytes accessed | tf_op | source)
XLA Modules:
  0.0 208.8 jit_solution(8808109054230232622)
XLA Ops:
  0.6 200.8 %attend.1 = (bf16[4,4,32,64,128]{4,3,2,1,0:T(8,128)(2,1)}, bf16[4,4,64,32,128]{4,3,2,1,0:T(8,128)(2,1)}, bf16[32,64,512]{2,1,0:T(8,128)(2,1)}, bf16[32,64,512]{2...) custom-call(bf16[32,64,512]{2,1,0:T(8,128)(2,1)} %q_in.1, bf16[32,64,512]{2,1,0:T(8,128)(2,1)} %k_in.1, ...), custom_call_target="tpu_custom_call" | custom-call | tf_op jit(solution)/shard_map/attend/pallas_call | solution.py:489
  201.4 7.3 %add_parts.1 = (bf16[32,64,512]{2,1,0:T(8,128)(2,1)}, bf16[32,64,512]{2,1,0:T(8,128)(2,1)}, bf16[32,64,512]{2,1,0:T(8,128)(2,1)}, bf16[32,64,512]{2,1,0:T(8,128)(2,1)}) custom-call(bf16[4,4,32,64,128]{4,3,2,1,0:T(8,128)(2,1)} %get-tuple-element.14.row_back, bf16[4,4,64,32,128]{4,3,2,1,0:T(8,128)(2,1)} %get-tuple-element.15.col_back, ...), custom_call_target="tpu_custom_call" | custom-call | tf_op jit(solution)/shard_map/add_parts/pallas_call | solution.py:529

commit v6 on v5

--- a/solution.py
+++ b/solution.py
@@ -93,9 +93,11 @@
     perm[...] = swap_matrix()
     st[...] = jnp.zeros_like(st)
     lt[...] = jnp.zeros_like(lt)
-    for copy in load(0):
+    first_load = load(0)
+    first_load[0].wait()
+    turn(0, 0)
+    for copy in first_load[1:]:
         copy.wait()
-    turn(0, 0)
     pl.semaphore_wait(barrier, NC + NR - 2)
 
     def send_in(h):

time: 209 us -> 209 us (level)
  no operation moved by 1% of the time
where the time goes in v6:
time: 209 us
  Pallas kernels  208 us (100%)
    pallas_call x1, Pallas kernels, shards(): pl.pallas_call(kernel, out_shape=backs + (out,) * 4, in_specs=[any_spec]...  201 us
    pallas_call x1, Pallas kernels, shards(): pl.pallas_call(add_kernel, out_shape=(out,) * 4, in_specs=[any_spec] * 6,...  7.35 us

profile of v6, /device:TPU:8, one launch (start us, length us, event | category | flops | bytes accessed | tf_op | source)
XLA Modules:
  0.0 208.8 jit_solution(11029701710496997887)
XLA Ops:
  0.6 200.8 %attend.1 = (bf16[4,4,32,64,128]{4,3,2,1,0:T(8,128)(2,1)}, bf16[4,4,64,32,128]{4,3,2,1,0:T(8,128)(2,1)}, bf16[32,64,512]{2,1,0:T(8,128)(2,1)}, bf16[32,64,512]{2...) custom-call(bf16[32,64,512]{2,1,0:T(8,128)(2,1)} %q_in.1, bf16[32,64,512]{2,1,0:T(8,128)(2,1)} %k_in.1, ...), custom_call_target="tpu_custom_call" | custom-call | tf_op jit(solution)/shard_map/attend/pallas_call | solution.py:491
  201.4 7.3 %add_parts.1 = (bf16[32,64,512]{2,1,0:T(8,128)(2,1)}, bf16[32,64,512]{2,1,0:T(8,128)(2,1)}, bf16[32,64,512]{2,1,0:T(8,128)(2,1)}, bf16[32,64,512]{2,1,0:T(8,128)(2,1)}) custom-call(bf16[4,4,32,64,128]{4,3,2,1,0:T(8,128)(2,1)} %get-tuple-element.14.row_back, bf16[4,4,64,32,128]{4,3,2,1,0:T(8,128)(2,1)} %get-tuple-element.15.col_back, ...), custom_call_target="tpu_custom_call" | custom-call | tf_op jit(solution)/shard_map/add_parts/pallas_call | solution.py:531
